TPU v7x, 256 devices: a whole 4x4x8 slice. The times are simulated.
256 devices in a mesh: rep: 8 (over z_hi, y), fsdp: 32 (over z_lo, x, core).
Axes of the slice: x: 4, y: 4, z: 8 (z_hi: 2, z_lo: 4; z = z_hi * 4 + z_lo), core: 2. Of those that a mesh axis runs over, the one named last changes fastest.
Arguments:
- acts: bfloat16 [8, 8192, 7168], P('rep', 'fsdp'), may hold values from -6 to 6
- key_weight: bfloat16 [8, 7168, 512], P('rep', 'fsdp'), may hold values from -0.0625 to 0.0625
- cotangent: bfloat16 [8, 8192, 512], P('rep', 'fsdp'), may hold values from -6 to 6
- frag_local: bfloat16 [8, 7168, 1024], P('rep', 'fsdp'), may hold values from -6 to 6
- frag_anchor: float32 [7168, 1024], P('fsdp', 'rep'), may hold values from -6 to 6
- frag_moment: float32 [7168, 1024], P('fsdp', 'rep'), may hold values from -6 to 6
- frag_pending: float32 [7168, 1024], P('fsdp', 'rep'), may hold values from -6 to 6
Outputs:
- keys: bfloat16 [8, 8192, 512], P('rep', 'fsdp')
- key_grad: bfloat16 [8, 7168, 512], P('rep', 'fsdp')
- act_grad: bfloat16 [8, 8192, 7168], P('rep', 'fsdp')
- local_next: bfloat16 [8, 7168, 1024], P('rep', 'fsdp')
- anchor_next: float32 [7168, 1024], P('fsdp', 'rep')
- moment_next: float32 [7168, 1024], P('fsdp', 'rep')
- pending_next: float32 [7168, 1024], P('fsdp', 'rep')
All inputs are finite; a program needn't handle non-finite values.
Results may differ from a plain program's by a relative error of at most 0.012.
Values may be sent and summed in bfloat16 or wider, within the bound.
A program may use at most 128 MiB of HBM per device.

v0:
```python
import jax
import jax.numpy as jnp
from jax import lax
from jax.sharding import PartitionSpec as P


def outer_update(anchor, moment, pending, local_sum, replicas):
    pending_next = anchor - local_sum / replicas
    moment_next = 0.9 * moment + pending
    anchor_next = anchor - 0.7 * (pending + 0.9 * moment_next)
    return (pending_next, moment_next, anchor_next)


def on_device(acts, key_weight, cotangent, frag_local, frag_anchor, frag_moment, frag_pending):
    inputs = acts[0]
    weight = key_weight[0]
    cot = cotangent[0]
    whole = lax.all_gather(weight, "fsdp", axis=0, tiled=True)
    keys = jnp.dot(inputs, whole, preferred_element_type=jnp.float32)
    back = lax.dot_general(cot, whole, (((1,), (1,)), ((), ())), preferred_element_type=jnp.float32)
    summed = lax.psum_scatter(
        lax.dot_general(inputs, cot, (((0,), (0,)), ((), ())), preferred_element_type=jnp.float32),
        "fsdp",
        scatter_dimension=0,
        tiled=True,
    )
    group_tokens = inputs.shape[0] * lax.axis_size("fsdp")
    grad = (summed * group_tokens ** (-0.5)).astype(jnp.bfloat16)
    local = frag_local[0]
    local_float = local.astype(jnp.float32)
    replicas = lax.axis_size("rep")
    width = frag_anchor.shape[1]
    local_sum = lax.psum(local_float.astype(jnp.bfloat16), "rep").astype(jnp.float32)
    anchor_all, moment_all, pending_all = (
        lax.all_gather(frag_anchor, "rep", axis=1, tiled=True),
        lax.all_gather(frag_moment, "rep", axis=1, tiled=True),
        lax.all_gather(frag_pending, "rep", axis=1, tiled=True),
    )
    pending_full, moment_full, anchor_full = outer_update(
        anchor_all, moment_all, pending_all, local_sum, replicas
    )
    shared = anchor_full.astype(jnp.bfloat16).astype(jnp.float32)
    local_next = (0.5 * local_float + 0.5 * shared).astype(jnp.bfloat16)
    offset = lax.axis_index("rep") * width
    pending_next = lax.dynamic_slice_in_dim(pending_full, offset, width, 1)
    moment_next = lax.dynamic_slice_in_dim(moment_full, offset, width, 1)
    anchor_next = lax.dynamic_slice_in_dim(anchor_full, offset, width, 1)
    return (
        keys.astype(jnp.bfloat16)[None],
        grad[None],
        back.astype(jnp.bfloat16)[None],
        local_next[None],
        anchor_next,
        moment_next,
        pending_next,
    )


def solution(mesh):
    placed = (
        P("rep", "fsdp", None),
        P("rep", "fsdp", None),
        P("rep", "fsdp", None),
        P("rep", "fsdp", None),
        P("fsdp", "rep"),
        P("fsdp", "rep"),
        P("fsdp", "rep"),
    )
    return jax.shard_map(
        on_device,
        mesh=mesh,
        in_specs=placed,
        out_specs=(
            P("rep", "fsdp", None),
            P("rep", "fsdp", None),
            P("rep", "fsdp", None),
            P("rep", "fsdp", None),
            P("fsdp", "rep"),
            P("fsdp", "rep"),
            P("fsdp", "rep"),
        ),
        check_vma=False,
    )
```

profile of v0, /device:TPU:8, one launch (start us, length us, event | category | flops | bytes accessed | tf_op | source)
XLA Modules:
  0.0 407.9 jit_solution(4273775027867722196)
XLA Ops:
  8.0 0.0 copy-start
  8.0 49.1 %all_gather.13 = f32[224,1024]{1,0:T(8,128)S(1)} all-gather(f32[224,128]{1,0:T(8,128)} %param.11), channel_id=1, replica_groups=mesh['rep'=8,'fsdp'=32] {'rep'}, dimensions={1}, use_global_device_ids=true | all-gather | bytes 1032192 | tf_op jit(solution)/shard_map/all_gather | solution.py:35
  57.1 47.3 %all_gather.15 = f32[224,1024]{1,0:T(8,128)S(1)} all-gather(f32[224,128]{1,0:T(8,128)} %param.12), channel_id=1, replica_groups=mesh['rep'=8,'fsdp'=32] {'rep'}, dimensions={1}, use_global_device_ids=true | all-gather | bytes 1032192 | tf_op jit(solution)/shard_map/all_gather | solution.py:36
  104.3 46.5 %all_gather.14 = f32[224,1024]{1,0:T(8,128)S(1)} all-gather(f32[224,128]{1,0:T(8,128)} %param.13), channel_id=1, replica_groups=mesh['rep'=8,'fsdp'=32] {'rep'}, dimensions={1}, use_global_device_ids=true | all-gather | bytes 1032192 | tf_op jit(solution)/shard_map/all_gather | solution.py:37
  150.8 2.2 fusion.17
  153.0 0.0 all-reduce.2.cloned.1.call-start
  153.0 0.7 all-reduce.2.cloned.1.call-update
  153.7 0.0 all-gather.3.cloned.1.call-start
  153.8 0.5 all-gather.3.cloned.1.call-update
  154.3 0.0 reduce-scatter.2.cloned.1.call-start
  154.3 0.0 copy-done
  154.3 9.3 %fusion.4 = f32[7168,512]{1,0:T(8,128)} fusion(bf16[1,256,7168]{2,1,0:T(8,128)(2,1)} %param.7, bf16[1,256,512]{2,1,0:T(8,128)(2,1)S(1)} %copy-done), kind=kOutput, calls=%fused_computation.5 | convolution fusion | flops 1879048192 | bytes 18612224 | tf_op jit(solution)/shard_map/dot_general | solution.py:22
  163.7 0.0 reduce-scatter.2.cloned.1.call-update
  163.7 0.7 constant_dynamic-slice_fusion
  164.4 102.4 %all-reduce.2.cloned.1.call-done = bf16[224,1024]{1,0:T(8,128)(2,1)} async-done(((bf16[224,1024]{1,0:T(8,128)(2,1)}), bf16[224,1024]{1,0:T(8,128)(2,1)}) %all-reduce.2.cloned.1.call-update) | async-done | bytes 458768 | tf_op jit(solution)/shard_map/psum | solution.py:33
  266.8 1.5 dynamic-slice_subtract_fusion
  268.3 0.0 all-gather.3.cloned.1.call-done
  268.3 0.0 copy-start.1
  268.3 0.0 copy-start.2
  268.3 7.3 %fusion = bf16[1,256,7168]{2,1,0:T(8,128)(2,1)} fusion(bf16[1,7168,512]{2,1,0:T(8,128)(2,1)} %all-gather.3.cloned.1.call-done, bf16[1,256,512]{2,1,0:T(8,128)(2,1)S(1)} %copy-done), kind=kOutput, calls=%fused_computation.1 | convolution fusion | flops 1880883200 | bytes 11272192 | tf_op jit(solution)/shard_map/dot_general | solution.py:20
  275.6 0.0 copy-done.1
  275.6 0.0 copy-done.2
  275.6 2.8 fusion.12
  278.4 120.4 %reduce-scatter.2.cloned.1.call-done = f32[224,512]{1,0:T(8,128)} async-done(((f32[7168,512]{1,0:T(8,128)}), f32[224,512]{1,0:T(8,128)}) %reduce-scatter.2.cloned.1.call-update) | async-done | bytes 458768 | tf_op jit(solution)/shard_map/reduce_scatter | solution.py:21
  398.8 1.7 fusion.20
Async XLA Ops:
  8.0 146.3 %copy-start = (bf16[1,256,512]{2,1,0:T(8,128)(2,1)S(1)}, bf16[1,256,512]{2,1,0:T(8,128)(2,1)}, u32[]{:S(2)}) copy-start(bf16[1,256,512]{2,1,0:T(8,128)(2,1)} %param.9) | copy-start | bytes 786436
  153.0 113.8 %all-reduce.2.cloned.1.call-start = ((), (), s32[]{:S(2)}) async-start(), calls=%async_computation.2 | async-start | bytes 917504 | tf_op jit(solution)/shard_map/psum | solution.py:33
  153.7 114.6 %all-gather.3.cloned.1.call-start = ((), (), s32[]{:S(2)}) async-start(), calls=%async_computation.3 | async-start | bytes 7569408 | tf_op jit(solution)/shard_map/all_gather | solution.py:18
  154.3 244.5 %reduce-scatter.2.cloned.1.call-start = ((), (), s32[]{:S(2)}) async-start(), calls=%async_computation.1 | async-start | bytes 15138816 | tf_op jit(solution)/shard_map/reduce_scatter | solution.py:21
  268.3 7.3 %copy-start.1 = (bf16[1,7168,512]{2,1,0:T(8,128)(2,1)S(1)}, bf16[1,7168,512]{2,1,0:T(8,128)(2,1)}, u32[]{:S(2)}) copy-start(bf16[1,7168,512]{2,1,0:T(8,128)(2,1)} %all-gather.3.cloned.1.call-done) | copy-start | bytes 22020100
  268.3 7.3 %copy-start.2 = (bf16[1,256,7168]{2,1,0:T(8,128)(2,1)S(1)}, bf16[1,256,7168]{2,1,0:T(8,128)(2,1)}, u32[]{:S(2)}) copy-start(bf16[1,256,7168]{2,1,0:T(8,128)(2,1)} %param.7) | copy-start | bytes 11010052
Sparse Core Ops, SparseCore 0:
  156.4 110.3 all-reduce.1
Sparse Core Ops, SparseCore 1:
  156.0 71.0 all-gather.2
  229.5 169.2 reduce-scatter.1
where the time goes:
time: 409 us; the launch traced here: 408 us
  waiting for transfers between devices  224 us (55%)
  blocking collectives  143 us (35%)
  matrix products  19.4 us (5%)
  between operations  15.5 us (4%)
  other arithmetic  5.4 us (1%)
    reduce_scatter x1, waiting for transfers between devices, on_device(): lax.psum_scatter(lax.dot_general(inputs, cot, (((0,), (0,)), ((), ())), p...  120 us
    psum x1, waiting for transfers between devices, on_device(): lax.psum(local_float.astype(jnp.bfloat16), 'rep').astype(jnp.float32)  102 us
    all_gather x1, blocking collectives, on_device(): lax.all_gather(frag_anchor, 'rep', axis=1, tiled=True)  49.1 us
    all_gather x1, blocking collectives, on_device(): lax.all_gather(frag_moment, 'rep', axis=1, tiled=True)  47.3 us
    all_gather x1, blocking collectives, on_device(): lax.all_gather(frag_pending, 'rep', axis=1, tiled=True)  46.5 us
    dot_general x1, matrix products, on_device(): lax.dot_general(inputs, cot, (((0,), (0,)), ((), ())), preferred_element_...  9.34 us
  transfers between devices with their start and end apart: 3, of which 2 were waited for; matrix products, arithmetic and copies ran while one was open for 5% of the time, Pallas kernels for 0%

commit v1 on v0

v1 whole, which is shorter than its diff:
```python
import functools

import jax
import jax.numpy as jnp
from jax import lax
from jax.experimental import pallas as pl
from jax.experimental.pallas import tpu as pltpu
from jax.sharding import PartitionSpec as P

MESH = pl.DeviceIdType.MESH
BF = jnp.bfloat16
F32 = jnp.float32

TOK = 256
D = 7168
KW = 512
FW = 1024
SH = 224
CH = 896
COLS = 128
GROUP_TOKENS = 8192
A1 = 160
A2 = SH - A1
R1 = 160
R2 = SH - R1
A1H, A2H = 80, 32
R1H, R2H = 80, 32

COUNTS = (
    ("a1z", 8), ("a1x", 16), ("a2x", 4), ("a2z", 32), ("sib", 8), ("dp", 8),
    ("r1h", 8), ("r1f", 8), ("r1z", 8), ("r2z", 32), ("r2h", 2), ("r2f", 2),
    ("oy", 6), ("os", 1), ("oy2", 3), ("oy3", 3), ("op", 1),
)
BASE = {}
TOTAL = 0
for _name, _n in COUNTS:
    BASE[_name] = TOTAL
    TOTAL += _n
LOADS = 7
ORDER = None


def default_order():
    o = []
    o += ["own", "outer_send"]
    o += [("dw", 0), ("dw", 1), "a2L", "a2R", ("dw", 2), ("dw", 3), ("z1", 1), ("x1L", 0), ("x1R", 0)]
    o += [("pair", 0), ("pair", 1), ("r1a", 0), ("dw", 4), ("dw", 5), "outer_y"]
    o += [("pair", 2), ("pair", 3), ("r1a", 1), "a2F", ("dw", 6), ("dw", 7)]
    o += [("z1", 2), ("x1L", 1), ("x1R", 1)]
    o += [("z2", 1, 0), ("z2", 1, 1), ("z2", 1, 2), ("z2", 1, 3)]
    o += [("pair", 4), ("pair", 5), ("r1a", 2), ("pair", 6), ("pair", 7), ("r1a", 3)]
    o += [("r2z", 0, 0), ("r2z", 0, 1), ("r2z", 0, 2), ("r2z", 0, 3)]
    o += [("x1F", 0), ("sibown", 0)]
    o += [("r1b", 0), ("z1", 3), ("x1L", 2), ("x1R", 2), ("r2z", 1, 0), ("r2z", 1, 1), ("r2z", 1, 2), ("r2z", 1, 3)]
    o += [("comp", 0), ("z2", 2, 0), ("z2", 2, 1), ("z2", 2, 2), ("z2", 2, 3)]
    o += [("r1b", 1), ("r1c", 0), "outer_mid", ("x1F", 1), ("sib", 1)]
    o += [("r2z", 2, 0), ("r2z", 2, 1), ("r2z", 2, 2), ("r2z", 2, 3), ("x1L", 3), ("x1R", 3), ("comp", 1)]
    o += [("r1b", 2), ("r1c", 1), ("x1F", 2), ("sib", 2)]
    o += [("z2", 3, 0), ("z2", 3, 1), ("z2", 3, 2), ("z2", 3, 3)]
    o += [("r2z", 3, 0), ("r2z", 3, 1), ("r2z", 3, 2), ("r2z", 3, 3), "r2a", ("r1b", 3), ("comp", 2)]
    o += [("r1c", 2), "r2b", ("x1F", 3), ("sib", 3), "outer_end", ("r1c", 3), "r2c", ("comp", 3)]
    return o


def kernel(
    acts_h, kw_h, cot_h, fl_h, anchor_h, moment_h, pending_h,
    keys_o, grad_o, back_o, local_o, anchor_o, moment_o, pending_o,
    acts, cot, fl, anchor, moment, pending,
    w, d, rb, r1h, r1f, r1z, r2z, r2h, r2f,
    acc, back, keys_v, grad_v, local_v, anchor_v, moment_v, pending_v,
    ry, shared, part_out, part_in,
    send_sem, recv_sem, load_sem, out_sem,
):
    rep, me = lax.axis_index("rep"), lax.axis_index("fsdp")
    zh, y = rep // 4, rep % 4
    z, x, c = me // 8, (me // 2) % 4, me % 2
    xl, xr, xo = (x + 3) % 4, (x + 1) % 4, (x + 2) % 4
    at_z0, at_z1, at_z2, at_z3 = z == 0, z == 1, z == 2, z == 3
    low, high = z == 0, z == 3

    def table(a, b, e, f):
        return jnp.where(at_z0, a, jnp.where(at_z1, b, jnp.where(at_z2, e, f)))

    near = [z, table(1, 0, 3, 2), table(2, 2, 1, 1), table(3, 3, 0, 0)]
    far = near[::-1]

    def dev(tz, tx, tc):
        return (rep, tz * 8 + tx * 2 + tc)

    right, left = dev(z, xr, c), dev(z, xl, c)
    up, down = dev(jnp.minimum(z + 1, 3), x, c), dev(jnp.maximum(z - 1, 0), x, c)
    sibling = dev(z, x, 1 - c)
    other_zh = ((1 - zh) * 4 + y, me)

    def chip(tz, tx):
        return tz * 4 + tx

    pending_sends = []

    def remote(src, dst, name, index, to):
        return pltpu.make_async_remote_copy(
            src_ref=src, dst_ref=dst,
            send_sem=send_sem.at[BASE[name] + index], recv_sem=recv_sem.at[BASE[name] + index],
            device_id=to, device_id_type=MESH,
        )

    def send(src, dst, name, index, to, when=None):
        copy = remote(src, dst, name, index, to)
        if when is None:
            copy.start()
        else:
            pl.when(when)(copy.start)
        pending_sends.append((copy, when))

    def recv(dst, name, index, when=None):
        copy = remote(dst, dst, name, index, sibling)
        if when is None:
            copy.wait_recv()
        else:
            pl.when(when)(copy.wait_recv)

    loads = [
        (kw_h, w.at[chip(z, x), c]), (cot_h, cot), (acts_h, acts), (fl_h, fl),
        (anchor_h, anchor), (moment_h, moment), (pending_h, pending),
    ]
    loads = [pltpu.make_async_copy(s, t, load_sem.at[i]) for i, (s, t) in enumerate(loads)]
    for copy in loads:
        copy.start()

    barrier = pltpu.get_barrier_semaphore()

    def greet(to):
        pl.semaphore_signal(barrier, inc=1, device_id=to, device_id_type=MESH)

    for to in (left, right, sibling, other_zh):
        greet(to)
    for k in range(1, 4):
        greet((zh * 4 + (y + k) % 4, me))

    @pl.when(z < 3)
    def _():
        greet(up)

    @pl.when(z > 0)
    def _():
        greet(down)

    loads[0].wait()
    pl.semaphore_wait(barrier, 8 + jnp.where(low | high, 0, 1))

    not_low, not_high = z > 0, z < 3

    def wr(tz, tx, start, size):
        return w.at[chip(tz, tx), c, pl.ds(start, size)]

    def a1_round(tz):
        for i, to in ((0, right), (1, left)):
            send(wr(tz, x, 0, A1), wr(tz, x, 0, A1), "a1x", tz * 4 + i, to)

    def a2_along(tz, tx, ups, downs):
        for i, to, ok in ((0, up, ups), (1, down, downs)):
            send(wr(tz, tx, A1, A2), wr(tz, tx, A1, A2), "a2z", (i * 4 + tz) * 4 + tx, to, ok)

    def own():
        for i, to in ((0, right), (1, left)):
            send(wr(z, x, A1, A2), wr(z, x, A1, A2), "a2x", i, to)
        for i, to, ok in ((0, up, not_high), (1, down, not_low)):
            send(wr(z, x, 0, A1), wr(z, x, 0, A1), "a1z", i * 4 + z, to, ok)
        a1_round(z)
        a2_along(z, x, not_high, not_low)

    def z1(j):
        tz = near[j]
        rising = tz < z
        recv(wr(tz, x, 0, A1), "a1z", jnp.where(rising, 0, 4) + tz)
        piece = wr(tz, x, 0, A1)
        send(piece, piece, "a1z", tz, up, rising & not_high)
        send(piece, piece, "a1z", 4 + tz, down, (tz > z) & not_low)
        a1_round(tz)

    def x1L(j):
        tz = near[j]
        recv(wr(tz, xl, 0, A1), "a1x", tz * 4)
        piece = wr(tz, xl, 0, A1H)
        send(piece, piece, "a1x", tz * 4 + 2, right)

    def x1R(j):
        tz = near[j]
        recv(wr(tz, xr, 0, A1), "a1x", tz * 4 + 1)
        piece = wr(tz, xr, A1H, A1 - A1H)
        send(piece, piece, "a1x", tz * 4 + 3, left)

    def x1F(j):
        tz = near[j]
        recv(wr(tz, xo, 0, A1H), "a1x", tz * 4 + 2)
        recv(wr(tz, xo, A1H, A1 - A1H), "a1x", tz * 4 + 3)

    def a2L():
        recv(wr(z, xl, A1, A2), "a2x", 0)
        piece = wr(z, xl, A1, A2H)
        send(piece, piece, "a2x", 2, right)
        a2_along(z, xl, not_high, not_low)

    def a2R():
        recv(wr(z, xr, A1, A2), "a2x", 1)
        piece = wr(z, xr, A1 + A2H, A2 - A2H)
        send(piece, piece, "a2x", 3, left)
        a2_along(z, xr, not_high, not_low)

    def a2F():
        recv(wr(z, xo, A1, A2H), "a2x", 2)
        recv(wr(z, xo, A1 + A2H, A2 - A2H), "a2x", 3)
        a2_along(z, xo, not_high, not_low)

    def z2(j, p):
        tz, tx = near[j], (x, xl, xr, xo)[p]
        rising = tz < z
        recv(wr(tz, tx, A1, A2), "a2z", (jnp.where(rising, 0, 4) + tz) * 4 + tx)
        a2_along(tz, tx, rising & not_high, (tz > z) & not_low)

    def half_of(j, p):
        tz, px = near[j], x // 2 if p == 0 else 1 - x // 2
        return tz * 2 + px, chip(tz, px * 2)

    def sib(j):
        for p in range(2):
            index, first = half_of(j, p)
            piece = w.at[pl.ds(first, 2), c]
            send(piece, piece, "sib", index, sibling)

    def comp(j):
        for p in range(2):
            index, first = half_of(j, p)
            recv(w.at[pl.ds(first, 2), 1 - c], "sib", index)
            col = pl.multiple_of(index * CH, CH)
            rows = w[pl.ds(first, 2)].reshape(CH, KW)
            got = jnp.dot(acts[:, pl.ds(col, CH)], rows, preferred_element_type=F32)
            if j == 0 and p == 0:
                acc[...] = got
            else:
                acc[...] += got
            back[:, pl.ds(col, CH)] = lax.dot_general(
                cot[...], rows, (((1,), (1,)), ((), ())), preferred_element_type=F32
            ).astype(BF)
            out = pltpu.make_async_copy(
                back.at[:, pl.ds(col, CH)], back_o.at[:, pl.ds(col, CH)], out_sem.at[j * 2 + p]
            )
            out.start()
            outs.append(out)

    outs = []

    def grad_chunk(n):
        tz, px = far[n // 2], 1 - x // 2 if n % 2 == 0 else x // 2
        return tz * 2 + px, chip(tz, px * 2)

    def dw(n):
        if n == 0:
            loads[1].wait()
            loads[2].wait()
        index, first = grad_chunk(n)
        col = pl.multiple_of(index * CH, CH)
        got = lax.dot_general(
            acts[:, pl.ds(col, CH)], cot[...], (((0,), (0,)), ((), ())), preferred_element_type=F32
        )
        d[pl.ds(first, 2)] = got.astype(BF).reshape(2, 2, SH, KW)
        send(d.at[pl.ds(first, 2), 1 - c], rb.at[pl.ds(first, 2)], "dp", index, sibling)

    def pair(n):
        index, first = grad_chunk(n)
        recv(rb.at[pl.ds(first, 2)], "dp", index)
        for k in range(2):
            d[first + k, c] = (d[first + k, c].astype(F32) + rb[first + k].astype(F32)).astype(BF)

    def add(tz, tx, start, size, *others):
        here = (chip(tz, tx), c, pl.ds(start, size))
        total = d[here].astype(F32)
        for ref in others:
            total = total + ref[...].astype(F32)
        d[here] = total.astype(BF)

    def dr(tz, tx, start, size):
        return d.at[chip(tz, tx), c, pl.ds(start, size)]

    def r1a(i):
        tz = far[i]
        send(dr(tz, xo, 0, R1H), r1h.at[tz, 0, pl.ds(0, R1H)], "r1h", tz * 2, right)
        send(dr(tz, xo, R1H, R1 - R1H), r1h.at[tz, 1, pl.ds(0, R1 - R1H)], "r1h", tz * 2 + 1, left)

    def r1b(i):
        tz = far[i]
        from_left, from_right = r1h.at[tz, 0, pl.ds(0, R1H)], r1h.at[tz, 1, pl.ds(0, R1 - R1H)]
        recv(from_left, "r1h", tz * 2)
        add(tz, xr, 0, R1H, from_left)
        send(dr(tz, xr, 0, R1), r1f.at[tz, 0], "r1f", tz * 2, right)
        recv(from_right, "r1h", tz * 2 + 1)
        add(tz, xl, R1H, R1 - R1H, from_right)
        send(dr(tz, xl, 0, R1), r1f.at[tz, 1], "r1f", tz * 2 + 1, left)

    scale = GROUP_TOKENS ** -0.5

    def along(tz, tx, start, size, buffer, name, index, extra):
        rising = tz > z
        first = jnp.where(rising, low, high)
        got = buffer(jnp.where(rising, 0, 1))
        where = index(jnp.where(rising, 0, 1))

        @pl.when(first)
        def _():
            if extra:
                add(tz, tx, start, size, *extra)

        @pl.when(jnp.logical_not(first))
        def _():
            recv(got, name, where)
            add(tz, tx, start, size, got, *extra)

        piece = dr(tz, tx, start, size)
        send(piece, got, name, where, up, rising)
        send(piece, got, name, where, down, jnp.logical_not(rising))

    def end(tx, start, size, buffer, name, index, extra, store):
        for ok, places in ((low, (1,)), (high, (0,)), (not_low & not_high, (0, 1))):
            @pl.when(ok)
            def _():
                for i in places:
                    recv(buffer(i), name, index(i))
                total = d[chip(z, tx), c, pl.ds(start, size)].astype(F32)
                for ref in [buffer(i) for i in places] + extra:
                    total = total + ref[...].astype(F32)
                store(total)

    def r1c(i):
        tz = far[i]
        recv(r1f.at[tz, 0], "r1f", tz * 2)
        recv(r1f.at[tz, 1], "r1f", tz * 2 + 1)
        extra = [r1f.at[tz, 0], r1f.at[tz, 1]]

        def buffer(k):
            return r1z.at[k, tz]

        def index(k):
            return k * 4 + tz

        if i < 3:
            along(tz, x, 0, R1, buffer, "r1z", index, extra)
        else:
            def store(total):
                grad_v[pl.ds(0, R1)] = (total * scale).astype(BF)

            end(x, 0, R1, buffer, "r1z", index, extra, store)

    def r2z_step(i, p):
        tz, tx = far[i], (xo, xl, xr, x)[p]

        def buffer(k):
            return r2z.at[k, tz, tx]

        def index(k):
            return (k * 4 + tz) * 4 + tx

        if i < 3:
            along(tz, tx, R1, R2, buffer, "r2z", index, [])
        else:
            def store(total):
                d[chip(z, tx), c, pl.ds(R1, R2)] = total.astype(BF)

            end(tx, R1, R2, buffer, "r2z", index, [], store)

    def r2a():
        send(dr(z, xo, R1, R2H), r2h.at[0, pl.ds(0, R2H)], "r2h", 0, right)
        send(dr(z, xo, R1 + R2H, R2 - R2H), r2h.at[1, pl.ds(0, R2 - R2H)], "r2h", 1, left)

    def r2b():
        from_left, from_right = r2h.at[0, pl.ds(0, R2H)], r2h.at[1, pl.ds(0, R2 - R2H)]
        recv(from_left, "r2h", 0)
        add(z, xr, R1, R2H, from_left)
        send(dr(z, xr, R1, R2), r2f.at[0], "r2f", 0, right)
        recv(from_right, "r2h", 1)
        add(z, xl, R1 + R2H, R2 - R2H, from_right)
        send(dr(z, xl, R1, R2), r2f.at[1], "r2f", 1, left)

    def r2c():
        recv(r2f.at[0], "r2f", 0)
        recv(r2f.at[1], "r2f", 1)
        total = d[chip(z, x), c, pl.ds(R1, R2)].astype(F32) + r2f[0].astype(F32) + r2f[1].astype(F32)
        grad_v[pl.ds(R1, R2)] = (total * scale).astype(BF)

    def outer_send():
        for copy in loads[3:]:
            copy.wait()
        for k in range(1, 4):
            ty = (y + k) % 4
            for h in range(2):
                send(
                    fl.at[:, pl.ds(pl.multiple_of((h * 4 + ty) * COLS, COLS), COLS)],
                    ry.at[k - 1, h], "oy", (k - 1) * 2 + h, (zh * 4 + ty, me),
                )
        moment_next = 0.9 * moment[...] + pending[...]
        anchor_next = anchor[...] - 0.7 * (pending[...] + 0.9 * moment_next)
        moment_v[...] = moment_next
        anchor_v[...] = anchor_next
        shared[zh, y] = anchor_next.astype(BF)
        send(shared.at[zh, y], shared.at[zh, y], "os", 0, other_zh)
        for k in range(1, 4):
            ty = (y + k) % 4
            send(shared.at[zh, y], shared.at[zh, y], "oy2", k - 1, (zh * 4 + ty, me))

    def outer_y():
        for k in range(1, 4):
            for h in range(2):
                recv(ry.at[k - 1, h], "oy", (k - 1) * 2 + h)
        recv(shared.at[1 - zh, y], "os", 0)
        for k in range(1, 4):
            ty = (y + k) % 4
            send(shared.at[1 - zh, y], shared.at[1 - zh, y], "oy3", k - 1, (zh * 4 + ty, me))

        def local(h):
            total = fl[:, pl.ds(pl.multiple_of((h * 4 + y) * COLS, COLS), COLS)].astype(F32)
            for k in range(3):
                total = total + ry[k, h].astype(F32)
            return total

        part_out[...] = local(1 - zh).astype(BF)
        send(part_out, part_in, "op", 0, other_zh)
        pending_v[...] = local(zh)

    def outer_mid():
        recv(part_in, "op", 0)
        pending_v[...] = anchor[...] - (pending_v[...] + part_in[...].astype(F32)) / 8

    def outer_end():
        for k in range(1, 4):
            ty = (y + 4 - k) % 4
            recv(shared.at[zh, ty], "oy2", k - 1)
            recv(shared.at[1 - zh, ty], "oy3", k - 1)
        for h in range(2):
            for q in range(4):
                cols = pl.ds((h * 4 + q) * COLS, COLS)
                local_v[:, cols] = (0.5 * fl[:, cols].astype(F32) + 0.5 * shared[h, q].astype(F32)).astype(BF)

    actions = {
        "own": own, "z1": z1, "x1L": x1L, "x1R": x1R, "x1F": x1F, "a2L": a2L, "a2R": a2R, "a2F": a2F,
        "z2": z2, "sib": sib, "sibown": sib, "comp": comp, "dw": dw, "pair": pair, "r1a": r1a, "r1b": r1b, "r1c": r1c,
        "r2z": r2z_step, "r2a": r2a, "r2b": r2b, "r2c": r2c,
        "outer_send": outer_send, "outer_y": outer_y, "outer_mid": outer_mid, "outer_end": outer_end,
    }
    for item in ORDER or default_order():
        name, *args = item if isinstance(item, tuple) else (item,)
        actions[name](*args)

    keys_v[...] = acc[...].astype(BF)
    for i, (s, t) in enumerate((
        (keys_v, keys_o), (grad_v, grad_o), (local_v, local_o),
        (anchor_v, anchor_o), (moment_v, moment_o), (pending_v, pending_o),
    )):
        out = pltpu.make_async_copy(s, t, out_sem.at[8 + i])
        out.start()
        outs.append(out)
    for out in outs:
        out.wait()
    for copy, when in pending_sends:
        if when is None:
            copy.wait_send()
        else:
            pl.when(when)(copy.wait_send)


def on_device(acts, key_weight, cotangent, frag_local, anchor, moment, pending):
    any_space = pl.BlockSpec(memory_space=pl.ANY)
    vm = pltpu.VMEM
    outs = pl.pallas_call(
        kernel,
        out_shape=[
            jax.ShapeDtypeStruct((TOK, KW), BF), jax.ShapeDtypeStruct((SH, KW), BF),
            jax.ShapeDtypeStruct((TOK, D), BF), jax.ShapeDtypeStruct((SH, FW), BF),
            jax.ShapeDtypeStruct((SH, COLS), F32), jax.ShapeDtypeStruct((SH, COLS), F32),
            jax.ShapeDtypeStruct((SH, COLS), F32),
        ],
        in_specs=[any_space] * 7,
        out_specs=[any_space] * 7,
        scratch_shapes=[
            vm((TOK, D), BF), vm((TOK, KW), BF), vm((SH, FW), BF),
            vm((SH, COLS), F32), vm((SH, COLS), F32), vm((SH, COLS), F32),
            vm((16, 2, SH, KW), BF), vm((16, 2, SH, KW), BF), vm((16, SH, KW), BF),
            vm((4, 2, max(R1H, R1 - R1H), KW), BF), vm((4, 2, R1, KW), BF), vm((2, 4, R1, KW), BF),
            vm((2, 4, 4, R2, KW), BF), vm((2, max(R2H, R2 - R2H), KW), BF), vm((2, R2, KW), BF),
            vm((TOK, KW), F32), vm((TOK, D), BF), vm((TOK, KW), BF), vm((SH, KW), BF), vm((SH, FW), BF),
            vm((SH, COLS), F32), vm((SH, COLS), F32), vm((SH, COLS), F32),
            vm((3, 2, SH, COLS), BF), vm((2, 4, SH, COLS), BF), vm((SH, COLS), BF), vm((SH, COLS), BF),
            pltpu.SemaphoreType.DMA((TOTAL,)), pltpu.SemaphoreType.DMA((TOTAL,)),
            pltpu.SemaphoreType.DMA((LOADS,)), pltpu.SemaphoreType.DMA((14,)),
        ],
        name="window",
        compiler_params=pltpu.CompilerParams(
            collective_id=1, has_side_effects=True, vmem_limit_bytes=56 * 2**20
        ),
    )(acts[0], key_weight[0], cotangent[0], frag_local[0], anchor, moment, pending)
    keys, grad, back, local, anchor_next, moment_next, pending_next = outs
    return (keys[None], grad[None], back[None], local[None], anchor_next, moment_next, pending_next)


def solution(mesh):
    wide, flat = P("rep", "fsdp", None), P("fsdp", "rep")
    return jax.shard_map(
        on_device,
        mesh=mesh,
        in_specs=(wide,) * 4 + (flat,) * 3,
        out_specs=(wide,) * 4 + (flat,) * 3,
        check_vma=False,
    )
```

time: 409 us -> 91.6 us (0.22)
  waiting for transfers between devices: 224 us -> 0 us
  blocking collectives: 143 us -> 0 us
  Pallas kernels: 0 us -> 80.5 us
  matrix products: 19.4 us -> 0 us
  between operations: 15.5 us -> 0.65 us
  local copies, waits for them, and re-layouts: 0.74 us -> 10.2 us
  other arithmetic: 5.4 us -> 0 us
    all_gather x3 -> x0, blocking collectives: 143 us -> none  [the longest x1 49.1 us: on_device(): lax.all_gather(frag_anchor, 'rep', axis=1, tiled=True)]
    reduce_scatter x1 -> x0, waiting for transfers between devices: 120 us -> none  [on_device(): lax.psum_scatter(lax.dot_general(inputs, cot, (((0,), (0,)), ((), ())), p...]
    psum x1 -> x0, waiting for transfers between devices: 102 us -> none  [on_device(): lax.psum(local_float.astype(jnp.bfloat16), 'rep').astype(jnp.float32)]
    pallas_call x0 -> x1, Pallas kernels: none -> 80.5 us  [on_device(): pl.pallas_call(kernel, out_shape=[jax.ShapeDtypeStruct((TOK, KW), BF), ja...]
    dot_general x3 -> x0, matrix products: 19.4 us -> none  [the longest x1 9.34 us: on_device(): lax.dot_general(inputs, cot, (((0,), (0,)), ((), ())), preferred_element_...]
    unnamed x6 -> x15, local copies, waits for them, and re-layouts: 0.02 us -> 10.2 us
  transfers between devices with their start and end apart: 3 -> 0, of which waited for: 2 -> 0; matrix products, arithmetic and copies ran while one was open for 5% -> 0% of each run, Pallas kernels for 0% -> 0%
where the time goes in v1:
time: 91.6 us; the launch traced here: 91.4 us
  Pallas kernels  80.5 us (88%)
  local copies, waits for them, and re-layouts  10.2 us (11%)
    pallas_call x1, Pallas kernels, on_device(): pl.pallas_call(kernel, out_shape=[jax.ShapeDtypeStruct((TOK, KW), BF), ja...  80.5 us
    unnamed x15, local copies, waits for them, and re-layouts  10.2 us

profile of v1, /device:TPU:8, one launch (start us, length us, event | category | flops | bytes accessed | tf_op | source)
XLA Modules:
  0.0 91.4 jit_solution(8777428458462044481)
XLA Ops:
  0.6 80.5 %window.1 = (bf16[256,512]{1,0:T(8,128)(2,1)}, bf16[224,512]{1,0:T(8,128)(2,1)}, bf16[256,7168]{1,0:T(8,128)(2,1)}, bf16[224,1024]{1,0:T(8,128)(2,1)}, f32[224,1...) custom-call(bf16[256,7168]{1,0:T(8,128)(2,1)} %bitcast.9, bf16[224,512]{1,0:T(8,128)(2,1)} %bitcast.15, ...), custom_call_target="tpu_custom_call" | custom-call | tf_op jit(solution)/shard_map/window/pallas_call | solution.py:472
  81.2 1.7 %copy.21 = bf16[1,256,512]{2,1,0:T(8,128)(2,1)} copy(bf16[1,256,512]{2,1,0:T(8,128)(2,1)} %bitcast.13) | data formatting | bytes 524288
  82.8 1.6 %copy.22 = bf16[1,224,512]{2,1,0:T(8,128)(2,1)} copy(bf16[1,224,512]{2,1,0:T(8,128)(2,1)} %bitcast.14) | data formatting | bytes 458752
  84.5 0.0 copy-start
  84.5 0.0 copy-start.3
  84.5 0.0 copy-start.2
  84.5 0.0 copy-start.1
  84.5 4.2 %copy.23 = bf16[1,256,7168]{2,1,0:T(8,128)(2,1)} copy(bf16[1,256,7168]{2,1,0:T(8,128)(2,1)} %bitcast.8) | data formatting | bytes 7340032
  88.7 0.0 copy-done
  88.7 0.8 copy.24
  89.4 0.0 copy-done.3
  89.4 0.6 copy.25
  90.1 0.0 copy-done.2
  90.1 0.6 copy.26
  90.7 0.0 copy-done.1
  90.7 0.6 copy.27
Async XLA Ops:
  84.5 4.2 %copy-start = (bf16[224,1024]{1,0:T(8,128)(2,1)S(1)}, bf16[224,1024]{1,0:T(8,128)(2,1)}, u32[]{:S(2)}) copy-start(bf16[224,1024]{1,0:T(8,128)(2,1)} %get-tuple-element.17) | copy-start | bytes 1376260
  84.5 5.0 %copy-start.3 = (f32[224,128]{1,0:T(8,128)S(1)}, f32[224,128]{1,0:T(8,128)}, u32[]{:S(2)}) copy-start(f32[224,128]{1,0:T(8,128)} %get-tuple-element.32) | copy-start | bytes 344068
  84.5 5.6 %copy-start.2 = (f32[224,128]{1,0:T(8,128)S(1)}, f32[224,128]{1,0:T(8,128)}, u32[]{:S(2)}) copy-start(f32[224,128]{1,0:T(8,128)} %get-tuple-element.33) | copy-start | bytes 344068
  84.5 6.3 %copy-start.1 = (f32[224,128]{1,0:T(8,128)S(1)}, f32[224,128]{1,0:T(8,128)}, u32[]{:S(2)}) copy-start(f32[224,128]{1,0:T(8,128)} %get-tuple-element.34) | copy-start | bytes 344068

commit v2 on v0

v2 whole, which is shorter than its diff:
```python
import functools

import jax
import jax.numpy as jnp
from jax import lax
from jax.experimental import pallas as pl
from jax.experimental.pallas import tpu as pltpu
from jax.sharding import PartitionSpec as P

MESH = pl.DeviceIdType.MESH
BF = jnp.bfloat16
F32 = jnp.float32

TOK = 256
D = 7168
KW = 512
FW = 1024
SH = 224
CH = 896
COLS = 128
GROUP_TOKENS = 8192

COUNTS = (
    ("a1z", 8), ("a1x", 16), ("a2x", 4), ("a2z", 32), ("sib", 8), ("dp", 8),
    ("r1h", 8), ("r1f", 8), ("r1z", 8), ("r2z", 32), ("r2h", 2), ("r2f", 2),
    ("oy", 6), ("os", 1), ("oy2", 3), ("oy3", 3), ("op", 1),
)
BASE = {}
TOTAL = 0
for _name, _n in COUNTS:
    BASE[_name] = TOTAL
    TOTAL += _n
LOADS = 7


ENDS = (
    ("own",), ("dw", 0), ("dw", 2), ("pair", 0), ("dw", 3), ("outer_send",), ("r1a", 0), ("dw", 1), ("a2L",),
    ("pair", 2), ("a2R",), ("pair", 3), ("dw", 4), ("dw", 5), ("z1", 1), ("r1a", 1), ("pair", 1), ("r2z", 1, 0),
    ("r2z", 0, 0), ("r1bL", 0), ("x1L", 0), ("pair", 4), ("x1R", 0), ("r2z", 0, 3), ("r2z", 0, 2), ("a2F",),
    ("x1L", 1), ("z2", 1, 0), ("r2z", 1, 3), ("sib", 0, 0), ("r2z", 1, 1), ("r1a", 2), ("r2z", 1, 2), ("r2z", 0, 1),
    ("x1R", 1), ("outer_y",), ("z2", 1, 1), ("z2", 2, 0), ("r1bR", 0), ("dw", 6), ("z1", 2), ("pair", 6), ("z1", 3),
    ("outer_mid",), ("comp", 0, 0), ("x1F", 1), ("pair", 5), ("z2", 1, 3), ("r2z", 2, 1), ("dw", 7), ("x1L", 2),
    ("r2z", 2, 0), ("r1bR", 1), ("r1bL", 1), ("z2", 1, 2), ("r1c", 0), ("r1a", 3), ("r1bL", 2), ("x1F", 0),
    ("x1L", 3), ("r2z", 2, 2), ("z2", 2, 2), ("z2", 2, 1), ("sib", 1, 1), ("x1R", 2), ("sib", 2, 0), ("z2", 2, 3),
    ("outer_end",), ("pair", 7), ("r1c", 1), ("sib", 1, 0), ("r1bR", 2), ("sib", 0, 1), ("r2z", 3, 0), ("r2a",),
    ("r1bL", 3), ("comp", 1, 1), ("z2", 3, 0), ("comp", 1, 0), ("r2z", 2, 3), ("x1F", 2), ("z2", 3, 1),
    ("sib", 2, 1), ("x1R", 3), ("z2", 3, 3), ("comp", 2, 0), ("r2z", 3, 2), ("r1bR", 3), ("z2", 3, 2), ("r1c", 2),
    ("comp", 0, 1), ("comp", 2, 1), ("sib", 3, 0), ("r2bL",), ("r2z", 3, 1), ("x1F", 3), ("r2bR",), ("sib", 3, 1),
    ("comp", 3, 0), ("comp", 3, 1), ("r2z", 3, 3), ("r1c", 3), ("r2c",),
)
MIDDLE = (
    ("own",), ("dw", 4), ("outer_send",), ("dw", 0), ("dw", 2), ("a2R",), ("dw", 6), ("a2L",), ("z1", 1), ("z1", 2),
    ("dw", 5), ("pair", 2), ("pair", 0), ("pair", 5), ("z2", 2, 0), ("z2", 2, 1), ("r1a", 0), ("r1a", 1),
    ("z2", 1, 2), ("z2", 1, 0), ("x1R", 1), ("a2F",), ("outer_y",), ("z2", 1, 1), ("dw", 3), ("dw", 1), ("x1L", 1),
    ("pair", 4), ("z1", 3), ("r2z", 1, 0), ("x1L", 0), ("pair", 6), ("r2z", 0, 0), ("z2", 3, 0), ("dw", 7),
    ("pair", 1), ("r2z", 0, 2), ("sib", 1, 0), ("x1R", 2), ("outer_end",), ("x1R", 0), ("z2", 1, 3), ("sib", 0, 0),
    ("r1bR", 0), ("outer_mid",), ("x1F", 1), ("z2", 2, 3), ("x1L", 3), ("r2z", 0, 3), ("z2", 2, 2), ("z2", 3, 1),
    ("pair", 3), ("r1a", 2), ("comp", 0, 0), ("z2", 3, 2), ("x1L", 2), ("r2z", 2, 0), ("r2z", 1, 3), ("r1bL", 0),
    ("pair", 7), ("x1F", 0), ("r2z", 1, 2), ("r2z", 2, 2), ("r2z", 1, 1), ("sib", 1, 1), ("r1bL", 1), ("r2z", 0, 1),
    ("x1F", 2), ("r1a", 3), ("sib", 0, 1), ("r1bR", 1), ("sib", 2, 1), ("r1bR", 2), ("r2z", 3, 0), ("r2z", 2, 3),
    ("x1R", 3), ("z2", 3, 3), ("r2a",), ("sib", 3, 0), ("comp", 1, 0), ("r1bR", 3), ("comp", 0, 1), ("sib", 2, 0),
    ("r1c", 0), ("r1bL", 2), ("r2z", 2, 1), ("r1bL", 3), ("comp", 1, 1), ("comp", 2, 1), ("comp", 3, 0), ("r1c", 1),
    ("r1c", 2), ("r2z", 3, 1), ("r2z", 3, 2), ("x1F", 3), ("comp", 2, 0), ("r2bR",), ("r2bL",), ("sib", 3, 1),
    ("r1c", 3), ("r2z", 3, 3), ("comp", 3, 1), ("r2c",),
)
ORDER = (ENDS, MIDDLE)


def kernel(
    order, A1, R1, acts_h, kw_h, cot_h, fl_h, anchor_h, moment_h, pending_h,
    keys_o, grad_o, back_o, local_o, anchor_o, moment_o, pending_o,
    acts, cot, fl, anchor, moment, pending,
    w, d, rb, r1h, r1f, r1z, r2z, r2h, r2f,
    acc, ry, shared, part_out, part_in,
    send_sem, recv_sem, load_sem,
):
    A2, R2 = SH - A1, SH - R1
    A1H, A2H, R1H, R2H = (n // 32 * 16 for n in (A1, A2, R1, R2))
    rep, me = lax.axis_index("rep"), lax.axis_index("fsdp")
    zh, y = rep // 4, rep % 4
    z, x, c = me // 8, (me // 2) % 4, me % 2
    xl, xr, xo = (x + 3) % 4, (x + 1) % 4, (x + 2) % 4
    at_z0, at_z1, at_z2, at_z3 = z == 0, z == 1, z == 2, z == 3
    low, high = z == 0, z == 3

    def table(a, b, e, f):
        return jnp.where(at_z0, a, jnp.where(at_z1, b, jnp.where(at_z2, e, f)))

    near = [z, table(1, 0, 3, 2), table(2, 2, 1, 1), table(3, 3, 0, 0)]
    far = near[::-1]

    def dev(tz, tx, tc):
        return (rep, tz * 8 + tx * 2 + tc)

    right, left = dev(z, xr, c), dev(z, xl, c)
    up, down = dev(jnp.minimum(z + 1, 3), x, c), dev(jnp.maximum(z - 1, 0), x, c)
    sibling = dev(z, x, 1 - c)
    other_zh = ((1 - zh) * 4 + y, me)

    def chip(tz, tx):
        return tz * 4 + tx

    pending_sends = []

    def remote(src, dst, name, index, to):
        return pltpu.make_async_remote_copy(
            src_ref=src, dst_ref=dst,
            send_sem=send_sem.at[BASE[name] + index], recv_sem=recv_sem.at[BASE[name] + index],
            device_id=to, device_id_type=MESH,
        )

    def send(src, dst, name, index, to):
        copy = remote(src, dst, name, index, to)
        copy.start()
        pending_sends.append(copy)

    def recv(dst, name, index):
        remote(dst, dst, name, index, sibling).wait_recv()

    loads = [
        (kw_h, w.at[chip(z, x), c]), (cot_h, cot), (acts_h, acts), (fl_h, fl),
        (anchor_h, anchor), (moment_h, moment), (pending_h, pending),
    ]
    loads = [pltpu.make_async_copy(s, t, load_sem.at[i]) for i, (s, t) in enumerate(loads)]
    for copy in loads:
        copy.start()

    barrier = pltpu.get_barrier_semaphore()

    def greet(to):
        pl.semaphore_signal(barrier, inc=1, device_id=to, device_id_type=MESH)

    for to in (left, right, sibling, other_zh):
        greet(to)
    for k in range(1, 4):
        greet((zh * 4 + (y + k) % 4, me))

    @pl.when(z < 3)
    def _():
        greet(up)

    @pl.when(z > 0)
    def _():
        greet(down)

    loads[0].wait()
    pl.semaphore_wait(barrier, 8 + jnp.where(low | high, 0, 1))

    inner = dev(jnp.where(low, 1, 2), x, c)

    def body(is_middle, order):
        def wr(tz, tx, start, size):
            return w.at[chip(tz, tx), c, pl.ds(start, size)]

        def a1_round(tz):
            for i, to in ((0, right), (1, left)):
                send(wr(tz, x, 0, A1), wr(tz, x, 0, A1), "a1x", tz * 4 + i, to)

        pending_sends.clear()
        tokens_here = []
        starts = ((0, up), (1, down)) if is_middle else ((jnp.where(low, 0, 1), inner),)

        def onward(tz):
            rising = tz < z
            return jnp.where(rising, 0, 1), dev(jnp.where(rising, z + 1, z - 1), x, c)

        def a2_along(tz, tx, ways):
            for i, to in ways:
                send(wr(tz, tx, A1, A2), wr(tz, tx, A1, A2), "a2z", (i * 4 + tz) * 4 + tx, to)

        def own():
            for i, to in ((0, right), (1, left)):
                send(wr(z, x, A1, A2), wr(z, x, A1, A2), "a2x", i, to)
            for i, to in starts:
                send(wr(z, x, 0, A1), wr(z, x, 0, A1), "a1z", i * 4 + z, to)
            a1_round(z)
            a2_along(z, x, starts)

        def z1(j):
            tz = near[j]
            rising = tz < z
            recv(wr(tz, x, 0, A1), "a1z", jnp.where(rising, 0, 4) + tz)
            piece = wr(tz, x, 0, A1)
            if is_middle:
                way, to = onward(tz)
                send(piece, piece, "a1z", way * 4 + tz, to)
            a1_round(tz)

        def x1L(j):
            tz = near[j]
            recv(wr(tz, xl, 0, A1), "a1x", tz * 4)
            piece = wr(tz, xl, 0, A1H)
            send(piece, piece, "a1x", tz * 4 + 2, right)

        def x1R(j):
            tz = near[j]
            recv(wr(tz, xr, 0, A1), "a1x", tz * 4 + 1)
            piece = wr(tz, xr, A1H, A1 - A1H)
            send(piece, piece, "a1x", tz * 4 + 3, left)

        def x1F(j):
            tz = near[j]
            recv(wr(tz, xo, 0, A1H), "a1x", tz * 4 + 2)
            recv(wr(tz, xo, A1H, A1 - A1H), "a1x", tz * 4 + 3)

        def a2L():
            recv(wr(z, xl, A1, A2), "a2x", 0)
            piece = wr(z, xl, A1, A2H)
            send(piece, piece, "a2x", 2, right)
            a2_along(z, xl, starts)

        def a2R():
            recv(wr(z, xr, A1, A2), "a2x", 1)
            piece = wr(z, xr, A1 + A2H, A2 - A2H)
            send(piece, piece, "a2x", 3, left)
            a2_along(z, xr, starts)

        def a2F():
            recv(wr(z, xo, A1, A2H), "a2x", 2)
            recv(wr(z, xo, A1 + A2H, A2 - A2H), "a2x", 3)
            a2_along(z, xo, starts)

        def z2(j, p):
            tz, tx = near[j], (x, xl, xr, xo)[p]
            rising = tz < z
            recv(wr(tz, tx, A1, A2), "a2z", (jnp.where(rising, 0, 4) + tz) * 4 + tx)
            if is_middle:
                a2_along(tz, tx, (onward(tz),))

        def half_of(j, p):
            tz, px = near[j], x // 2 if p == 0 else 1 - x // 2
            return tz * 2 + px, chip(tz, px * 2)

        def sib(j, p):
            index, first = half_of(j, p)
            piece = w.at[pl.ds(first, 2), c]
            send(piece, piece, "sib", index, sibling)

        def await_tokens():
            if not tokens_here:
                loads[1].wait()
                loads[2].wait()
                tokens_here.append(True)

        def comp(j, p):
            await_tokens()
            index, first = half_of(j, p)
            recv(w.at[pl.ds(first, 2), 1 - c], "sib", index)
            col = pl.multiple_of(index * CH, CH)
            rows = w[pl.ds(first, 2)].reshape(CH, KW)
            got = jnp.dot(acts[:, pl.ds(col, CH)], rows, preferred_element_type=F32)
            if j == 0 and p == 0:
                acc[...] = got
            else:
                acc[...] += got
            back_o[:, pl.ds(col, CH)] = lax.dot_general(
                cot[...], rows, (((1,), (1,)), ((), ())), preferred_element_type=F32
            ).astype(BF)

        def grad_chunk(n):
            tz, px = far[n // 2], 1 - x // 2 if n % 2 == 0 else x // 2
            return tz * 2 + px, chip(tz, px * 2)

        def dw(n):
            await_tokens()
            index, first = grad_chunk(n)
            col = pl.multiple_of(index * CH, CH)
            got = lax.dot_general(
                acts[:, pl.ds(col, CH)], cot[...], (((0,), (0,)), ((), ())), preferred_element_type=F32
            )
            d[pl.ds(first, 2)] = got.astype(BF).reshape(2, 2, SH, KW)
            send(d.at[pl.ds(first, 2), 1 - c], rb.at[pl.ds(first, 2)], "dp", index, sibling)

        def pair(n):
            index, first = grad_chunk(n)
            recv(rb.at[pl.ds(first, 2)], "dp", index)
            for k in range(2):
                d[first + k, c] = (d[first + k, c].astype(F32) + rb[first + k].astype(F32)).astype(BF)

        def add(tz, tx, start, size, *others):
            here = (chip(tz, tx), c, pl.ds(start, size))
            total = d[here].astype(F32)
            for ref in others:
                total = total + ref[...].astype(F32)
            d[here] = total.astype(BF)

        def dr(tz, tx, start, size):
            return d.at[chip(tz, tx), c, pl.ds(start, size)]

        def r1a(i):
            tz = far[i]
            send(dr(tz, xo, 0, R1H), r1h.at[tz, 0, pl.ds(0, R1H)], "r1h", tz * 2, right)
            send(dr(tz, xo, R1H, R1 - R1H), r1h.at[tz, 1, pl.ds(0, R1 - R1H)], "r1h", tz * 2 + 1, left)

        def r1bL(i):
            tz = far[i]
            got = r1h.at[tz, 0, pl.ds(0, R1H)]
            recv(got, "r1h", tz * 2)
            add(tz, xr, 0, R1H, got)
            send(dr(tz, xr, 0, R1), r1f.at[tz, 0], "r1f", tz * 2, right)

        def r1bR(i):
            tz = far[i]
            got = r1h.at[tz, 1, pl.ds(0, R1 - R1H)]
            recv(got, "r1h", tz * 2 + 1)
            add(tz, xl, R1H, R1 - R1H, got)
            send(dr(tz, xl, 0, R1), r1f.at[tz, 1], "r1f", tz * 2 + 1, left)

        scale = GROUP_TOKENS ** -0.5

        def along(tz, tx, start, size, buffer, name, index, extra):
            rising = tz > z
            way = jnp.where(rising, 0, 1)
            got, where = buffer(way), index(way)
            if is_middle:
                recv(got, name, where)
                add(tz, tx, start, size, got, *extra)
            elif extra:
                add(tz, tx, start, size, *extra)
            to = dev(jnp.where(rising, z + 1, z - 1), x, c)
            send(dr(tz, tx, start, size), got, name, where, to)

        def end(tx, start, size, buffer, name, index, extra):
            ways = (0, 1) if is_middle else (jnp.where(low, 1, 0),)
            for i in ways:
                recv(buffer(i), name, index(i))
            total = d[chip(z, tx), c, pl.ds(start, size)].astype(F32)
            for ref in [buffer(i) for i in ways] + extra:
                total = total + ref[...].astype(F32)
            return total

        def r1c(i):
            tz = far[i]
            recv(r1f.at[tz, 0], "r1f", tz * 2)
            recv(r1f.at[tz, 1], "r1f", tz * 2 + 1)
            extra = [r1f.at[tz, 0], r1f.at[tz, 1]]

            def buffer(k):
                return r1z.at[k, tz]

            def index(k):
                return k * 4 + tz

            if i < 3:
                along(tz, x, 0, R1, buffer, "r1z", index, extra)
            else:
                total = end(x, 0, R1, buffer, "r1z", index, extra)
                grad_o[pl.ds(0, R1)] = (total * scale).astype(BF)

        def r2z_step(i, p):
            tz, tx = far[i], (xo, xl, xr, x)[p]

            def buffer(k):
                return r2z.at[k, tz, tx]

            def index(k):
                return (k * 4 + tz) * 4 + tx

            if i < 3:
                along(tz, tx, R1, R2, buffer, "r2z", index, [])
            else:
                total = end(tx, R1, R2, buffer, "r2z", index, [])
                d[chip(z, tx), c, pl.ds(R1, R2)] = total.astype(BF)

        def r2a():
            send(dr(z, xo, R1, R2H), r2h.at[0, pl.ds(0, R2H)], "r2h", 0, right)
            send(dr(z, xo, R1 + R2H, R2 - R2H), r2h.at[1, pl.ds(0, R2 - R2H)], "r2h", 1, left)

        def r2bL():
            got = r2h.at[0, pl.ds(0, R2H)]
            recv(got, "r2h", 0)
            add(z, xr, R1, R2H, got)
            send(dr(z, xr, R1, R2), r2f.at[0], "r2f", 0, right)

        def r2bR():
            got = r2h.at[1, pl.ds(0, R2 - R2H)]
            recv(got, "r2h", 1)
            add(z, xl, R1 + R2H, R2 - R2H, got)
            send(dr(z, xl, R1, R2), r2f.at[1], "r2f", 1, left)

        def r2c():
            recv(r2f.at[0], "r2f", 0)
            recv(r2f.at[1], "r2f", 1)
            total = d[chip(z, x), c, pl.ds(R1, R2)].astype(F32) + r2f[0].astype(F32) + r2f[1].astype(F32)
            grad_o[pl.ds(R1, R2)] = (total * scale).astype(BF)

        def outer_send():
            for copy in loads[3:]:
                copy.wait()
            for k in range(1, 4):
                ty = (y + k) % 4
                for h in range(2):
                    send(
                        fl.at[:, pl.ds(pl.multiple_of((h * 4 + ty) * COLS, COLS), COLS)],
                        ry.at[k - 1, h], "oy", (k - 1) * 2 + h, (zh * 4 + ty, me),
                    )
            moment_next = 0.9 * moment[...] + pending[...]
            anchor_next = anchor[...] - 0.7 * (pending[...] + 0.9 * moment_next)
            moment_o[...] = moment_next
            anchor_o[...] = anchor_next
            shared[zh, y] = anchor_next.astype(BF)
            send(shared.at[zh, y], shared.at[zh, y], "os", 0, other_zh)
            for k in range(1, 4):
                ty = (y + k) % 4
                send(shared.at[zh, y], shared.at[zh, y], "oy2", k - 1, (zh * 4 + ty, me))

        def outer_y():
            for k in range(1, 4):
                for h in range(2):
                    recv(ry.at[k - 1, h], "oy", (k - 1) * 2 + h)
            recv(shared.at[1 - zh, y], "os", 0)
            for k in range(1, 4):
                ty = (y + k) % 4
                send(shared.at[1 - zh, y], shared.at[1 - zh, y], "oy3", k - 1, (zh * 4 + ty, me))

            def local(h):
                total = fl[:, pl.ds(pl.multiple_of((h * 4 + y) * COLS, COLS), COLS)].astype(F32)
                for k in range(3):
                    total = total + ry[k, h].astype(F32)
                return total

            part_out[...] = local(1 - zh).astype(BF)
            send(part_out, part_in, "op", 0, other_zh)
            pending_o[...] = local(zh)

        def outer_mid():
            recv(part_in, "op", 0)
            pending_o[...] = anchor[...] - (pending_o[...] + part_in[...].astype(F32)) / 8

        def outer_end():
            for k in range(1, 4):
                ty = (y + 4 - k) % 4
                recv(shared.at[zh, ty], "oy2", k - 1)
                recv(shared.at[1 - zh, ty], "oy3", k - 1)
            for h in range(2):
                for q in range(4):
                    cols = pl.ds((h * 4 + q) * COLS, COLS)
                    local_o[:, cols] = (0.5 * fl[:, cols].astype(F32) + 0.5 * shared[h, q].astype(F32)).astype(BF)

        actions = {
            "own": own, "z1": z1, "x1L": x1L, "x1R": x1R, "x1F": x1F, "a2L": a2L, "a2R": a2R, "a2F": a2F,
            "z2": z2, "sib": sib, "comp": comp, "dw": dw, "pair": pair, "r1a": r1a, "r1bL": r1bL, "r1bR": r1bR, "r1c": r1c,
            "r2z": r2z_step, "r2a": r2a, "r2bL": r2bL, "r2bR": r2bR, "r2c": r2c,
            "outer_send": outer_send, "outer_y": outer_y, "outer_mid": outer_mid, "outer_end": outer_end,
        }
        for name, *args in order:
            actions[name](*args)
        keys_o[...] = acc[...].astype(BF)
        for copy in pending_sends:
            copy.wait_send()

    pl.when(low | high)(functools.partial(body, False, order[0]))
    pl.when(jnp.logical_not(low | high))(functools.partial(body, True, order[1]))


def finish(*refs):
    sems = refs[-1]
    copies = [pltpu.make_async_copy(s, t, sems.at[i]) for i, (s, t) in enumerate(zip(refs[:7], refs[7:14], strict=True))]
    for copy in copies:
        copy.start()
    for copy in copies:
        copy.wait()


def launch(acts, key_weight, cotangent, frag_local, anchor, moment, pending, order=ORDER, A1=144, R1=144, name='window', cid=1):
    R2 = SH - R1
    R1H, R2H = R1 // 32 * 16, R2 // 32 * 16
    any_space = pl.BlockSpec(memory_space=pl.ANY)
    arrays = (acts[0], key_weight[0], cotangent[0], frag_local[0], anchor, moment, pending)
    vm = pltpu.VMEM
    outs = pl.pallas_call(
        functools.partial(kernel, order, A1, R1),
        out_shape=[
            vm((TOK, KW), BF), vm((SH, KW), BF), vm((TOK, D), BF), vm((SH, FW), BF),
            vm((SH, COLS), F32), vm((SH, COLS), F32), vm((SH, COLS), F32),
        ],
        in_specs=[any_space] * 7,
        out_specs=[pl.BlockSpec(memory_space=vm)] * 7,
        scratch_shapes=[
            vm((TOK, D), BF), vm((TOK, KW), BF), vm((SH, FW), BF),
            vm((SH, COLS), F32), vm((SH, COLS), F32), vm((SH, COLS), F32),
            vm((16, 2, SH, KW), BF), vm((16, 2, SH, KW), BF), vm((16, SH, KW), BF),
            vm((4, 2, max(R1H, R1 - R1H), KW), BF), vm((4, 2, R1, KW), BF), vm((2, 4, R1, KW), BF),
            vm((2, 4, 4, R2, KW), BF), vm((2, max(R2H, R2 - R2H), KW), BF), vm((2, R2, KW), BF),
            vm((TOK, KW), F32), vm((3, 2, SH, COLS), BF), vm((2, 4, SH, COLS), BF), vm((SH, COLS), BF), vm((SH, COLS), BF),
            pltpu.SemaphoreType.DMA((TOTAL,)), pltpu.SemaphoreType.DMA((TOTAL,)),
            pltpu.SemaphoreType.DMA((LOADS,)),
        ],
        name=name,
        compiler_params=pltpu.CompilerParams(
            collective_id=cid, has_side_effects=True, vmem_limit_bytes=46 * 2**20
        ),
    )(*[pltpu.with_memory_space_constraint(a, pltpu.HBM) for a in arrays])
    outs = pl.pallas_call(
        finish,
        out_shape=[jax.ShapeDtypeStruct(o.shape, o.dtype) for o in outs],
        in_specs=[any_space] * 7,
        out_specs=[any_space] * 7,
        scratch_shapes=[pltpu.SemaphoreType.DMA((7,))],
        name="finish",
        compiler_params=pltpu.CompilerParams(vmem_limit_bytes=2**20),
    )(*[pltpu.with_memory_space_constraint(o, vm) for o in outs])
    keys, grad, back, local, anchor_next, moment_next, pending_next = outs
    return (keys[None], grad[None], back[None], local[None], anchor_next, moment_next, pending_next)


def on_device(*arrays):
    return launch(*arrays)


def solution(mesh):
    wide, flat = P("rep", "fsdp", None), P("fsdp", "rep")
    return jax.shard_map(
        on_device,
        mesh=mesh,
        in_specs=(wide,) * 4 + (flat,) * 3,
        out_specs=(wide,) * 4 + (flat,) * 3,
        check_vma=False,
    )
```

time: 409 us -> 67.8 us (0.17)
  waiting for transfers between devices: 224 us -> 0 us
  blocking collectives: 143 us -> 0 us
  Pallas kernels: 0 us -> 66.2 us
  matrix products: 19.4 us -> 0 us
  between operations: 15.5 us -> 0.8 us
  other arithmetic: 5.4 us -> 0 us
    all_gather x3 -> x0, blocking collectives: 143 us -> none  [the longest x1 49.1 us: on_device(): lax.all_gather(frag_anchor, 'rep', axis=1, tiled=True)]
    reduce_scatter x1 -> x0, waiting for transfers between devices: 120 us -> none  [on_device(): lax.psum_scatter(lax.dot_general(inputs, cot, (((0,), (0,)), ((), ())), p...]
    psum x1 -> x0, waiting for transfers between devices: 102 us -> none  [on_device(): lax.psum(local_float.astype(jnp.bfloat16), 'rep').astype(jnp.float32)]
    pallas_call x0 -> x2, Pallas kernels: none -> 66.2 us  [the longest x1 63.9 us: launch(): pl.pallas_call(functools.partial(kernel, order, A1, R1), out_shape=[vm((T...]
    dot_general x3 -> x0, matrix products: 19.4 us -> none  [the longest x1 9.34 us: on_device(): lax.dot_general(inputs, cot, (((0,), (0,)), ((), ())), preferred_element_...]
  transfers between devices with their start and end apart: 3 -> 0, of which waited for: 2 -> 0; matrix products, arithmetic and copies ran while one was open for 5% -> 0% of each run, Pallas kernels for 0% -> 0%
where the time goes in v2:
time: 67.8 us; the launch traced here: 67 us
  Pallas kernels  66.2 us (98%)
  between operations  0.8 us (1%)
    pallas_call x1, Pallas kernels, launch(): pl.pallas_call(functools.partial(kernel, order, A1, R1), out_shape=[vm((T...  63.9 us
    pallas_call x1, Pallas kernels, launch(): pl.pallas_call(finish, out_shape=[jax.ShapeDtypeStruct(o.shape, o.dtype)...  2.3 us

profile of v2, /device:TPU:8, one launch (start us, length us, event | category | flops | bytes accessed | tf_op | source)
XLA Modules:
  0.0 67.0 jit_solution(15655355570443527176)
XLA Ops:
  0.6 63.9 %window.1 = (bf16[256,512]{1,0:T(8,128)(2,1)S(1)}, bf16[224,512]{1,0:T(8,128)(2,1)S(1)}, bf16[256,7168]{1,0:T(8,128)(2,1)S(1)}, bf16[224,1024]{1,0:T(8,128)(2,1)...) custom-call(bf16[256,7168]{1,0:T(8,128)(2,1)} %bitcast.8, ...), custom_call_target="tpu_custom_call" | custom-call | tf_op jit(solution)/shard_map/window/pallas_call | solution.py:471
  64.5 2.3 %finish.1 = (bf16[256,512]{1,0:T(8,128)(2,1)}, bf16[224,512]{1,0:T(8,128)(2,1)}, bf16[256,7168]{1,0:T(8,128)(2,1)}, bf16[224,1024]{1,0:T(8,128)(2,1)}, f32[224,1...) custom-call(bf16[256,512]{1,0:T(8,128)(2,1)S(1)} %get-tuple-element.21.refs_0_, ...), custom_call_target="tpu_custom_call" | custom-call | tf_op jit(solution)/shard_map/finish/pallas_call | solution.py:494

commit v3 on v2

--- a/solution.py
+++ b/solution.py
@@ -21,8 +21,8 @@
 GROUP_TOKENS = 8192
 
 COUNTS = (
-    ("a1z", 8), ("a1x", 16), ("a2x", 4), ("a2z", 32), ("sib", 8), ("dp", 8),
-    ("r1h", 8), ("r1f", 8), ("r1z", 8), ("r2z", 32), ("r2h", 2), ("r2f", 2),
+    ("a1z", 8), ("a1x", 16), ("a2x", 4), ("a2z", 16), ("sib", 8), ("dp", 8),
+    ("r1h", 8), ("r1f", 8), ("r1z", 8), ("r2z", 16), ("r2h", 2), ("r2f", 2),
     ("oy", 6), ("os", 1), ("oy2", 3), ("oy3", 3), ("op", 1),
 )
 BASE = {}
@@ -34,34 +34,32 @@
 
 
 ENDS = (
-    ("own",), ("dw", 0), ("dw", 2), ("pair", 0), ("dw", 3), ("outer_send",), ("r1a", 0), ("dw", 1), ("a2L",),
-    ("pair", 2), ("a2R",), ("pair", 3), ("dw", 4), ("dw", 5), ("z1", 1), ("r1a", 1), ("pair", 1), ("r2z", 1, 0),
-    ("r2z", 0, 0), ("r1bL", 0), ("x1L", 0), ("pair", 4), ("x1R", 0), ("r2z", 0, 3), ("r2z", 0, 2), ("a2F",),
-    ("x1L", 1), ("z2", 1, 0), ("r2z", 1, 3), ("sib", 0, 0), ("r2z", 1, 1), ("r1a", 2), ("r2z", 1, 2), ("r2z", 0, 1),
-    ("x1R", 1), ("outer_y",), ("z2", 1, 1), ("z2", 2, 0), ("r1bR", 0), ("dw", 6), ("z1", 2), ("pair", 6), ("z1", 3),
-    ("outer_mid",), ("comp", 0, 0), ("x1F", 1), ("pair", 5), ("z2", 1, 3), ("r2z", 2, 1), ("dw", 7), ("x1L", 2),
-    ("r2z", 2, 0), ("r1bR", 1), ("r1bL", 1), ("z2", 1, 2), ("r1c", 0), ("r1a", 3), ("r1bL", 2), ("x1F", 0),
-    ("x1L", 3), ("r2z", 2, 2), ("z2", 2, 2), ("z2", 2, 1), ("sib", 1, 1), ("x1R", 2), ("sib", 2, 0), ("z2", 2, 3),
-    ("outer_end",), ("pair", 7), ("r1c", 1), ("sib", 1, 0), ("r1bR", 2), ("sib", 0, 1), ("r2z", 3, 0), ("r2a",),
-    ("r1bL", 3), ("comp", 1, 1), ("z2", 3, 0), ("comp", 1, 0), ("r2z", 2, 3), ("x1F", 2), ("z2", 3, 1),
-    ("sib", 2, 1), ("x1R", 3), ("z2", 3, 3), ("comp", 2, 0), ("r2z", 3, 2), ("r1bR", 3), ("z2", 3, 2), ("r1c", 2),
-    ("comp", 0, 1), ("comp", 2, 1), ("sib", 3, 0), ("r2bL",), ("r2z", 3, 1), ("x1F", 3), ("r2bR",), ("sib", 3, 1),
-    ("comp", 3, 0), ("comp", 3, 1), ("r2z", 3, 3), ("r1c", 3), ("r2c",),
+    ("o2x",), ("o1z",), ("dw", 1), ("dw", 6), ("x1o", 0), ("dw", 2), ("dw", 0), ("dw", 5), ("a2L",), ("a2R",),
+    ("pair", 2), ("pair", 0), ("pair", 1), ("r1a", 0), ("r2z", 0, 0), ("dw", 4), ("r1a", 1), ("x1R", 0), ("x1L", 0),
+    ("z1", 1), ("pair", 4), ("r1bL", 0), ("x1o", 1), ("r2z", 0, 1), ("a2F",), ("outer_send",), ("dw", 3),
+    ("r1bR", 0), ("z1", 2), ("g2", 1), ("pair", 3), ("r2z", 1, 0), ("dw", 7), ("sib", 0, 0), ("z1", 3), ("pair", 6),
+    ("g2", 0), ("r1a", 2), ("pair", 5), ("x1o", 2), ("comp", 0, 0), ("outer_y",), ("r1bR", 1), ("x1L", 1),
+    ("r2z", 2, 0), ("x1R", 1), ("x1o", 3), ("r2z", 1, 1), ("r1bL", 1), ("outer_end",), ("x1L", 2), ("x1R", 2),
+    ("z2", 1, 1), ("pair", 7), ("z2", 1, 0), ("r1a", 3), ("x1F", 0), ("sib", 1, 0), ("x1F", 1), ("r1c", 0),
+    ("x1R", 3), ("r1bR", 2), ("x1L", 3), ("sib", 0, 1), ("comp", 1, 0), ("r2z", 3, 0), ("r2z", 2, 1), ("r2a",),
+    ("r1c", 1), ("z2", 2, 0), ("r1bL", 2), ("x1F", 2), ("r2z", 3, 1), ("z2", 2, 1), ("outer_mid",), ("sib", 2, 0),
+    ("sib", 2, 1), ("sib", 1, 1), ("x1F", 3), ("comp", 0, 1), ("r1bR", 3), ("z2", 3, 0), ("r1bL", 3), ("z2", 3, 1),
+    ("r1c", 2), ("sib", 3, 0), ("sib", 3, 1), ("comp", 1, 1), ("comp", 2, 1), ("r2bL",), ("r2bR",), ("comp", 3, 1),
+    ("comp", 2, 0), ("comp", 3, 0), ("r1c", 3), ("r2c",),
 )
 MIDDLE = (
-    ("own",), ("dw", 4), ("outer_send",), ("dw", 0), ("dw", 2), ("a2R",), ("dw", 6), ("a2L",), ("z1", 1), ("z1", 2),
-    ("dw", 5), ("pair", 2), ("pair", 0), ("pair", 5), ("z2", 2, 0), ("z2", 2, 1), ("r1a", 0), ("r1a", 1),
-    ("z2", 1, 2), ("z2", 1, 0), ("x1R", 1), ("a2F",), ("outer_y",), ("z2", 1, 1), ("dw", 3), ("dw", 1), ("x1L", 1),
-    ("pair", 4), ("z1", 3), ("r2z", 1, 0), ("x1L", 0), ("pair", 6), ("r2z", 0, 0), ("z2", 3, 0), ("dw", 7),
-    ("pair", 1), ("r2z", 0, 2), ("sib", 1, 0), ("x1R", 2), ("outer_end",), ("x1R", 0), ("z2", 1, 3), ("sib", 0, 0),
-    ("r1bR", 0), ("outer_mid",), ("x1F", 1), ("z2", 2, 3), ("x1L", 3), ("r2z", 0, 3), ("z2", 2, 2), ("z2", 3, 1),
-    ("pair", 3), ("r1a", 2), ("comp", 0, 0), ("z2", 3, 2), ("x1L", 2), ("r2z", 2, 0), ("r2z", 1, 3), ("r1bL", 0),
-    ("pair", 7), ("x1F", 0), ("r2z", 1, 2), ("r2z", 2, 2), ("r2z", 1, 1), ("sib", 1, 1), ("r1bL", 1), ("r2z", 0, 1),
-    ("x1F", 2), ("r1a", 3), ("sib", 0, 1), ("r1bR", 1), ("sib", 2, 1), ("r1bR", 2), ("r2z", 3, 0), ("r2z", 2, 3),
-    ("x1R", 3), ("z2", 3, 3), ("r2a",), ("sib", 3, 0), ("comp", 1, 0), ("r1bR", 3), ("comp", 0, 1), ("sib", 2, 0),
-    ("r1c", 0), ("r1bL", 2), ("r2z", 2, 1), ("r1bL", 3), ("comp", 1, 1), ("comp", 2, 1), ("comp", 3, 0), ("r1c", 1),
-    ("r1c", 2), ("r2z", 3, 1), ("r2z", 3, 2), ("x1F", 3), ("comp", 2, 0), ("r2bR",), ("r2bL",), ("sib", 3, 1),
-    ("r1c", 3), ("r2z", 3, 3), ("comp", 3, 1), ("r2c",),
+    ("o2x",), ("dw", 1), ("o1z",), ("dw", 0), ("outer_send",), ("x1o", 0), ("dw", 6), ("pair", 0), ("a2R",),
+    ("z1", 1), ("r1a", 0), ("x1o", 1), ("z1", 2), ("pair", 1), ("a2L",), ("x1L", 0), ("g2", 1), ("dw", 4),
+    ("z1", 3), ("r1bR", 0), ("x1R", 0), ("r2z", 0, 0), ("x1o", 3), ("dw", 7), ("r2z", 0, 1), ("z2", 2, 1),
+    ("dw", 5), ("a2F",), ("pair", 4), ("dw", 2), ("pair", 6), ("x1o", 2), ("sib", 0, 0), ("g2", 0), ("z2", 1, 1),
+    ("outer_y",), ("r1a", 2), ("pair", 7), ("pair", 2), ("dw", 3), ("pair", 5), ("x1L", 1), ("r1a", 1),
+    ("r2z", 2, 0), ("x1F", 0), ("z2", 2, 0), ("comp", 0, 0), ("z2", 1, 0), ("x1R", 1), ("pair", 3), ("r1bL", 0),
+    ("r1bR", 2), ("r1bL", 1), ("x1R", 3), ("x1R", 2), ("r2z", 1, 0), ("r1a", 3), ("x1L", 2), ("x1L", 3),
+    ("sib", 0, 1), ("r2z", 2, 1), ("comp", 0, 1), ("z2", 3, 0), ("r1bL", 2), ("r2z", 1, 1), ("r2z", 3, 0),
+    ("sib", 1, 0), ("r1bR", 1), ("z2", 3, 1), ("outer_end",), ("r2a",), ("sib", 3, 0), ("r1c", 0), ("x1F", 1),
+    ("x1F", 2), ("r1bL", 3), ("sib", 1, 1), ("comp", 1, 0), ("comp", 3, 0), ("x1F", 3), ("sib", 2, 0),
+    ("r2z", 3, 1), ("sib", 3, 1), ("r1bR", 3), ("comp", 1, 1), ("outer_mid",), ("r2bL",), ("r1c", 1), ("r1c", 2),
+    ("sib", 2, 1), ("comp", 2, 0), ("r2bR",), ("comp", 3, 1), ("comp", 2, 1), ("r1c", 3), ("r2c",),
 )
 ORDER = (ENDS, MIDDLE)
 
@@ -98,7 +96,7 @@
     other_zh = ((1 - zh) * 4 + y, me)
 
     def chip(tz, tx):
-        return tz * 4 + tx
+        return tz, tx // 2, tx % 2
 
     pending_sends = []
 
@@ -118,7 +116,7 @@
         remote(dst, dst, name, index, sibling).wait_recv()
 
     loads = [
-        (kw_h, w.at[chip(z, x), c]), (cot_h, cot), (acts_h, acts), (fl_h, fl),
+        (kw_h, w.at[(*chip(z, x), c)]), (cot_h, cot), (acts_h, acts), (fl_h, fl),
         (anchor_h, anchor), (moment_h, moment), (pending_h, pending),
     ]
     loads = [pltpu.make_async_copy(s, t, load_sem.at[i]) for i, (s, t) in enumerate(loads)]
@@ -150,7 +148,7 @@
 
     def body(is_middle, order):
         def wr(tz, tx, start, size):
-            return w.at[chip(tz, tx), c, pl.ds(start, size)]
+            return w.at[(*chip(tz, tx), c, pl.ds(start, size))]
 
         def a1_round(tz):
             for i, to in ((0, right), (1, left)):
@@ -164,27 +162,35 @@
             rising = tz < z
             return jnp.where(rising, 0, 1), dev(jnp.where(rising, z + 1, z - 1), x, c)
 
-        def a2_along(tz, tx, ways):
+        def two(tz, g):
+            return w.at[tz, :, (x + g) % 2, c, pl.ds(A1, A2)]
+
+        def a2_along(tz, g, ways):
             for i, to in ways:
-                send(wr(tz, tx, A1, A2), wr(tz, tx, A1, A2), "a2z", (i * 4 + tz) * 4 + tx, to)
-
-        def own():
+                send(two(tz, g), two(tz, g), "a2z", (i * 4 + tz) * 2 + g, to)
+
+        def o2x():
             for i, to in ((0, right), (1, left)):
                 send(wr(z, x, A1, A2), wr(z, x, A1, A2), "a2x", i, to)
+
+        def o1z():
             for i, to in starts:
                 send(wr(z, x, 0, A1), wr(z, x, 0, A1), "a1z", i * 4 + z, to)
-            a1_round(z)
-            a2_along(z, x, starts)
+
+        def g2(g):
+            a2_along(z, g, starts)
+
+        def x1o(j):
+            a1_round(near[j])
 
         def z1(j):
             tz = near[j]
             rising = tz < z
             recv(wr(tz, x, 0, A1), "a1z", jnp.where(rising, 0, 4) + tz)
-            piece = wr(tz, x, 0, A1)
             if is_middle:
+                piece = wr(tz, x, 0, A1)
                 way, to = onward(tz)
                 send(piece, piece, "a1z", way * 4 + tz, to)
-            a1_round(tz)
 
         def x1L(j):
             tz = near[j]
@@ -207,33 +213,29 @@
             recv(wr(z, xl, A1, A2), "a2x", 0)
             piece = wr(z, xl, A1, A2H)
             send(piece, piece, "a2x", 2, right)
-            a2_along(z, xl, starts)
 
         def a2R():
             recv(wr(z, xr, A1, A2), "a2x", 1)
             piece = wr(z, xr, A1 + A2H, A2 - A2H)
             send(piece, piece, "a2x", 3, left)
-            a2_along(z, xr, starts)
 
         def a2F():
             recv(wr(z, xo, A1, A2H), "a2x", 2)
             recv(wr(z, xo, A1 + A2H, A2 - A2H), "a2x", 3)
-            a2_along(z, xo, starts)
-
-        def z2(j, p):
-            tz, tx = near[j], (x, xl, xr, xo)[p]
-            rising = tz < z
-            recv(wr(tz, tx, A1, A2), "a2z", (jnp.where(rising, 0, 4) + tz) * 4 + tx)
+
+        def z2(j, g):
+            tz = near[j]
+            recv(two(tz, g), "a2z", (jnp.where(tz < z, 0, 4) + tz) * 2 + g)
             if is_middle:
-                a2_along(tz, tx, (onward(tz),))
+                a2_along(tz, g, (onward(tz),))
 
         def half_of(j, p):
             tz, px = near[j], x // 2 if p == 0 else 1 - x // 2
-            return tz * 2 + px, chip(tz, px * 2)
+            return tz * 2 + px, (tz, px)
 
         def sib(j, p):
             index, first = half_of(j, p)
-            piece = w.at[pl.ds(first, 2), c]
+            piece = w.at[(*first, slice(None), c)]
             send(piece, piece, "sib", index, sibling)
 
         def await_tokens():
@@ -245,9 +247,9 @@
         def comp(j, p):
             await_tokens()
             index, first = half_of(j, p)
-            recv(w.at[pl.ds(first, 2), 1 - c], "sib", index)
+            recv(w.at[(*first, slice(None), 1 - c)], "sib", index)
             col = pl.multiple_of(index * CH, CH)
-            rows = w[pl.ds(first, 2)].reshape(CH, KW)
+            rows = w[first].reshape(CH, KW)
             got = jnp.dot(acts[:, pl.ds(col, CH)], rows, preferred_element_type=F32)
             if j == 0 and p == 0:
                 acc[...] = got
@@ -259,7 +261,7 @@
 
         def grad_chunk(n):
             tz, px = far[n // 2], 1 - x // 2 if n % 2 == 0 else x // 2
-            return tz * 2 + px, chip(tz, px * 2)
+            return tz * 2 + px, (tz, px)
 
         def dw(n):
             await_tokens()
@@ -268,24 +270,24 @@
             got = lax.dot_general(
                 acts[:, pl.ds(col, CH)], cot[...], (((0,), (0,)), ((), ())), preferred_element_type=F32
             )
-            d[pl.ds(first, 2)] = got.astype(BF).reshape(2, 2, SH, KW)
-            send(d.at[pl.ds(first, 2), 1 - c], rb.at[pl.ds(first, 2)], "dp", index, sibling)
+            d[first] = got.astype(BF).reshape(2, 2, SH, KW)
+            send(d.at[(*first, slice(None), 1 - c)], rb.at[first], "dp", index, sibling)
 
         def pair(n):
             index, first = grad_chunk(n)
-            recv(rb.at[pl.ds(first, 2)], "dp", index)
+            recv(rb.at[first], "dp", index)
             for k in range(2):
-                d[first + k, c] = (d[first + k, c].astype(F32) + rb[first + k].astype(F32)).astype(BF)
+                d[(*first, k, c)] = (d[(*first, k, c)].astype(F32) + rb[(*first, k)].astype(F32)).astype(BF)
 
         def add(tz, tx, start, size, *others):
-            here = (chip(tz, tx), c, pl.ds(start, size))
+            here = (*chip(tz, tx), c, pl.ds(start, size))
             total = d[here].astype(F32)
             for ref in others:
                 total = total + ref[...].astype(F32)
             d[here] = total.astype(BF)
 
         def dr(tz, tx, start, size):
-            return d.at[chip(tz, tx), c, pl.ds(start, size)]
+            return d.at[(*chip(tz, tx), c, pl.ds(start, size))]
 
         def r1a(i):
             tz = far[i]
@@ -308,32 +310,36 @@
 
         scale = GROUP_TOKENS ** -0.5
 
-        def along(tz, tx, start, size, buffer, name, index, extra):
+        def gather_up(here, others):
+            total = d[here].astype(F32)
+            for ref in others:
+                total = total + ref[...].astype(F32)
+            return total
+
+        def along(tz, here, buffer, name, index, extra):
             rising = tz > z
             way = jnp.where(rising, 0, 1)
             got, where = buffer(way), index(way)
             if is_middle:
                 recv(got, name, where)
-                add(tz, tx, start, size, got, *extra)
+                d[here] = gather_up(here, [got, *extra]).astype(BF)
             elif extra:
-                add(tz, tx, start, size, *extra)
+                d[here] = gather_up(here, extra).astype(BF)
             to = dev(jnp.where(rising, z + 1, z - 1), x, c)
-            send(dr(tz, tx, start, size), got, name, where, to)
-
-        def end(tx, start, size, buffer, name, index, extra):
+            send(d.at[here], got, name, where, to)
+
+        def end(here, buffer, name, index, extra):
             ways = (0, 1) if is_middle else (jnp.where(low, 1, 0),)
             for i in ways:
                 recv(buffer(i), name, index(i))
-            total = d[chip(z, tx), c, pl.ds(start, size)].astype(F32)
-            for ref in [buffer(i) for i in ways] + extra:
-                total = total + ref[...].astype(F32)
-            return total
+            return gather_up(here, [buffer(i) for i in ways] + extra)
 
         def r1c(i):
             tz = far[i]
             recv(r1f.at[tz, 0], "r1f", tz * 2)
             recv(r1f.at[tz, 1], "r1f", tz * 2 + 1)
             extra = [r1f.at[tz, 0], r1f.at[tz, 1]]
+            here = (*chip(tz, x), c, pl.ds(0, R1))
 
             def buffer(k):
                 return r1z.at[k, tz]
@@ -342,25 +348,25 @@
                 return k * 4 + tz
 
             if i < 3:
-                along(tz, x, 0, R1, buffer, "r1z", index, extra)
+                along(tz, here, buffer, "r1z", index, extra)
             else:
-                total = end(x, 0, R1, buffer, "r1z", index, extra)
+                total = end(here, buffer, "r1z", index, extra)
                 grad_o[pl.ds(0, R1)] = (total * scale).astype(BF)
 
-        def r2z_step(i, p):
-            tz, tx = far[i], (xo, xl, xr, x)[p]
+        def r2z_step(i, g):
+            tz = far[i]
+            here = (tz, slice(None), (x + g) % 2, c, pl.ds(R1, R2))
 
             def buffer(k):
-                return r2z.at[k, tz, tx]
+                return r2z.at[k, tz, g]
 
             def index(k):
-                return (k * 4 + tz) * 4 + tx
+                return (k * 4 + tz) * 2 + g
 
             if i < 3:
-                along(tz, tx, R1, R2, buffer, "r2z", index, [])
+                along(tz, here, buffer, "r2z", index, [])
             else:
-                total = end(tx, R1, R2, buffer, "r2z", index, [])
-                d[chip(z, tx), c, pl.ds(R1, R2)] = total.astype(BF)
+                d[here] = end(here, buffer, "r2z", index, []).astype(BF)
 
         def r2a():
             send(dr(z, xo, R1, R2H), r2h.at[0, pl.ds(0, R2H)], "r2h", 0, right)
@@ -381,7 +387,7 @@
         def r2c():
             recv(r2f.at[0], "r2f", 0)
             recv(r2f.at[1], "r2f", 1)
-            total = d[chip(z, x), c, pl.ds(R1, R2)].astype(F32) + r2f[0].astype(F32) + r2f[1].astype(F32)
+            total = d[(*chip(z, x), c, pl.ds(R1, R2))].astype(F32) + r2f[0].astype(F32) + r2f[1].astype(F32)
             grad_o[pl.ds(R1, R2)] = (total * scale).astype(BF)
 
         def outer_send():
@@ -438,7 +444,7 @@
                     local_o[:, cols] = (0.5 * fl[:, cols].astype(F32) + 0.5 * shared[h, q].astype(F32)).astype(BF)
 
         actions = {
-            "own": own, "z1": z1, "x1L": x1L, "x1R": x1R, "x1F": x1F, "a2L": a2L, "a2R": a2R, "a2F": a2F,
+            "o2x": o2x, "o1z": o1z, "g2": g2, "x1o": x1o, "z1": z1, "x1L": x1L, "x1R": x1R, "x1F": x1F, "a2L": a2L, "a2R": a2R, "a2F": a2F,
             "z2": z2, "sib": sib, "comp": comp, "dw": dw, "pair": pair, "r1a": r1a, "r1bL": r1bL, "r1bR": r1bR, "r1c": r1c,
             "r2z": r2z_step, "r2a": r2a, "r2bL": r2bL, "r2bR": r2bR, "r2c": r2c,
             "outer_send": outer_send, "outer_y": outer_y, "outer_mid": outer_mid, "outer_end": outer_end,
@@ -455,7 +461,12 @@
 
 def finish(*refs):
     sems = refs[-1]
-    copies = [pltpu.make_async_copy(s, t, sems.at[i]) for i, (s, t) in enumerate(zip(refs[:7], refs[7:14], strict=True))]
+    pairs = []
+    for source, target in zip(refs[:7], refs[7:14], strict=True):
+        parts = 4 if source.shape[1] == D else 1
+        rows = source.shape[0] // parts
+        pairs += [(source.at[pl.ds(k * rows, rows)], target.at[pl.ds(k * rows, rows)]) for k in range(parts)]
+    copies = [pltpu.make_async_copy(s, t, sems.at[i]) for i, (s, t) in enumerate(pairs)]
     for copy in copies:
         copy.start()
     for copy in copies:
@@ -479,9 +490,9 @@
         scratch_shapes=[
             vm((TOK, D), BF), vm((TOK, KW), BF), vm((SH, FW), BF),
             vm((SH, COLS), F32), vm((SH, COLS), F32), vm((SH, COLS), F32),
-            vm((16, 2, SH, KW), BF), vm((16, 2, SH, KW), BF), vm((16, SH, KW), BF),
+            vm((4, 2, 2, 2, SH, KW), BF), vm((4, 2, 2, 2, SH, KW), BF), vm((4, 2, 2, SH, KW), BF),
             vm((4, 2, max(R1H, R1 - R1H), KW), BF), vm((4, 2, R1, KW), BF), vm((2, 4, R1, KW), BF),
-            vm((2, 4, 4, R2, KW), BF), vm((2, max(R2H, R2 - R2H), KW), BF), vm((2, R2, KW), BF),
+            vm((2, 4, 2, 2, R2, KW), BF), vm((2, max(R2H, R2 - R2H), KW), BF), vm((2, R2, KW), BF),
             vm((TOK, KW), F32), vm((3, 2, SH, COLS), BF), vm((2, 4, SH, COLS), BF), vm((SH, COLS), BF), vm((SH, COLS), BF),
             pltpu.SemaphoreType.DMA((TOTAL,)), pltpu.SemaphoreType.DMA((TOTAL,)),
             pltpu.SemaphoreType.DMA((LOADS,)),
@@ -496,7 +507,7 @@
         out_shape=[jax.ShapeDtypeStruct(o.shape, o.dtype) for o in outs],
         in_specs=[any_space] * 7,
         out_specs=[any_space] * 7,
-        scratch_shapes=[pltpu.SemaphoreType.DMA((7,))],
+        scratch_shapes=[pltpu.SemaphoreType.DMA((10,))],
         name="finish",
         compiler_params=pltpu.CompilerParams(vmem_limit_bytes=2**20),
     )(*[pltpu.with_memory_space_constraint(o, vm) for o in outs])

time: 67.8 us -> 65.3 us (0.963); the launches traced: 67 us -> 65.2 us
  Pallas kernels: 66.2 us -> 64.4 us
    pallas_call x1, Pallas kernels: 63.9 us -> 62.1 us  [launch(): pl.pallas_call(functools.partial(kernel, order, A1, R1), out_shape=[vm((T...]
where the time goes in v3:
time: 65.3 us; the launch traced here: 65.2 us
  Pallas kernels  64.4 us (99%)
  between operations  0.8 us (1%)
    pallas_call x1, Pallas kernels, launch(): pl.pallas_call(functools.partial(kernel, order, A1, R1), out_shape=[vm((T...  62.1 us
    pallas_call x1, Pallas kernels, launch(): pl.pallas_call(finish, out_shape=[jax.ShapeDtypeStruct(o.shape, o.dtype)...  2.33 us

profile of v3, /device:TPU:8, one launch (start us, length us, event | category | flops | bytes accessed | tf_op | source)
XLA Modules:
  0.0 65.2 jit_solution(6572575479656830163)
XLA Ops:
  0.6 62.1 %window.1 = (bf16[256,512]{1,0:T(8,128)(2,1)S(1)}, bf16[224,512]{1,0:T(8,128)(2,1)S(1)}, bf16[256,7168]{1,0:T(8,128)(2,1)S(1)}, bf16[224,1024]{1,0:T(8,128)(2,1)...) custom-call(bf16[256,7168]{1,0:T(8,128)(2,1)} %bitcast.8, ...), custom_call_target="tpu_custom_call" | custom-call | tf_op jit(solution)/shard_map/window/pallas_call | solution.py:482
  62.8 2.3 %finish.1 = (bf16[256,512]{1,0:T(8,128)(2,1)}, bf16[224,512]{1,0:T(8,128)(2,1)}, bf16[256,7168]{1,0:T(8,128)(2,1)}, bf16[224,1024]{1,0:T(8,128)(2,1)}, f32[224,1...) custom-call(bf16[256,512]{1,0:T(8,128)(2,1)S(1)} %get-tuple-element.21.refs_0_, ...), custom_call_target="tpu_custom_call" | custom-call | tf_op jit(solution)/shard_map/finish/pallas_call | solution.py:505

commit v4 on v3

--- a/solution.py
+++ b/solution.py
@@ -31,35 +31,36 @@
     BASE[_name] = TOTAL
     TOTAL += _n
 LOADS = 7
+LAG = 40
 
 
 ENDS = (
-    ("o2x",), ("o1z",), ("dw", 1), ("dw", 6), ("x1o", 0), ("dw", 2), ("dw", 0), ("dw", 5), ("a2L",), ("a2R",),
-    ("pair", 2), ("pair", 0), ("pair", 1), ("r1a", 0), ("r2z", 0, 0), ("dw", 4), ("r1a", 1), ("x1R", 0), ("x1L", 0),
-    ("z1", 1), ("pair", 4), ("r1bL", 0), ("x1o", 1), ("r2z", 0, 1), ("a2F",), ("outer_send",), ("dw", 3),
-    ("r1bR", 0), ("z1", 2), ("g2", 1), ("pair", 3), ("r2z", 1, 0), ("dw", 7), ("sib", 0, 0), ("z1", 3), ("pair", 6),
-    ("g2", 0), ("r1a", 2), ("pair", 5), ("x1o", 2), ("comp", 0, 0), ("outer_y",), ("r1bR", 1), ("x1L", 1),
-    ("r2z", 2, 0), ("x1R", 1), ("x1o", 3), ("r2z", 1, 1), ("r1bL", 1), ("outer_end",), ("x1L", 2), ("x1R", 2),
-    ("z2", 1, 1), ("pair", 7), ("z2", 1, 0), ("r1a", 3), ("x1F", 0), ("sib", 1, 0), ("x1F", 1), ("r1c", 0),
-    ("x1R", 3), ("r1bR", 2), ("x1L", 3), ("sib", 0, 1), ("comp", 1, 0), ("r2z", 3, 0), ("r2z", 2, 1), ("r2a",),
-    ("r1c", 1), ("z2", 2, 0), ("r1bL", 2), ("x1F", 2), ("r2z", 3, 1), ("z2", 2, 1), ("outer_mid",), ("sib", 2, 0),
-    ("sib", 2, 1), ("sib", 1, 1), ("x1F", 3), ("comp", 0, 1), ("r1bR", 3), ("z2", 3, 0), ("r1bL", 3), ("z2", 3, 1),
-    ("r1c", 2), ("sib", 3, 0), ("sib", 3, 1), ("comp", 1, 1), ("comp", 2, 1), ("r2bL",), ("r2bR",), ("comp", 3, 1),
-    ("comp", 2, 0), ("comp", 3, 0), ("r1c", 3), ("r2c",),
+    ("o2x",), ("dw", 0), ("o1z",), ("x1o", 0), ("dw", 2), ("dw", 1), ("dw", 7), ("a2R",), ("dw", 3), ("pair", 1),
+    ("pair", 0), ("a2L",), ("g2", 1), ("r1a", 0), ("pair", 2), ("pair", 7), ("dw", 6), ("pair", 3), ("x1R", 0),
+    ("r2z", 0, 0), ("outer_send",), ("z1", 1), ("x1L", 0), ("x1o", 1), ("r2z", 1, 0), ("pair", 6), ("r1bR", 0),
+    ("dw", 4), ("r1a", 1), ("a2F",), ("g2", 0), ("r2z", 1, 1), ("sib", 0, 0), ("z1", 2), ("r1bL", 0), ("x1F", 0),
+    ("r2z", 0, 1), ("x1L", 1), ("dw", 5), ("r1bL", 1), ("pair", 5), ("x1o", 2), ("r1c", 0), ("z1", 3), ("x1o", 3),
+    ("x1R", 1), ("pair", 4), ("x1R", 2), ("r2z", 2, 0), ("outer_y",), ("r2z", 2, 1), ("x1L", 2), ("r1bR", 1),
+    ("outer_end",), ("x1L", 3), ("z2", 1, 1), ("x1F", 1), ("r1a", 2), ("comp", 0, 0), ("z2", 2, 0), ("x1R", 3),
+    ("sib", 0, 1), ("z2", 2, 1), ("r1a", 3), ("sib", 2, 0), ("z2", 1, 0), ("x1F", 2), ("r1c", 1), ("r1bR", 2),
+    ("r1bL", 2), ("sib", 2, 1), ("r2z", 3, 0), ("z2", 3, 1), ("sib", 1, 0), ("r2a",), ("x1F", 3), ("z2", 3, 0),
+    ("r1bR", 3), ("r1bL", 3), ("comp", 2, 1), ("comp", 1, 0), ("sib", 3, 1), ("r2z", 3, 1), ("r2bL",), ("r1c", 2),
+    ("comp", 0, 1), ("outer_mid",), ("sib", 3, 0), ("r2bR",), ("sib", 1, 1), ("comp", 3, 1), ("comp", 2, 0),
+    ("comp", 3, 0), ("comp", 1, 1), ("r1c", 3), ("r2c",),
 )
 MIDDLE = (
-    ("o2x",), ("dw", 1), ("o1z",), ("dw", 0), ("outer_send",), ("x1o", 0), ("dw", 6), ("pair", 0), ("a2R",),
-    ("z1", 1), ("r1a", 0), ("x1o", 1), ("z1", 2), ("pair", 1), ("a2L",), ("x1L", 0), ("g2", 1), ("dw", 4),
-    ("z1", 3), ("r1bR", 0), ("x1R", 0), ("r2z", 0, 0), ("x1o", 3), ("dw", 7), ("r2z", 0, 1), ("z2", 2, 1),
-    ("dw", 5), ("a2F",), ("pair", 4), ("dw", 2), ("pair", 6), ("x1o", 2), ("sib", 0, 0), ("g2", 0), ("z2", 1, 1),
-    ("outer_y",), ("r1a", 2), ("pair", 7), ("pair", 2), ("dw", 3), ("pair", 5), ("x1L", 1), ("r1a", 1),
-    ("r2z", 2, 0), ("x1F", 0), ("z2", 2, 0), ("comp", 0, 0), ("z2", 1, 0), ("x1R", 1), ("pair", 3), ("r1bL", 0),
-    ("r1bR", 2), ("r1bL", 1), ("x1R", 3), ("x1R", 2), ("r2z", 1, 0), ("r1a", 3), ("x1L", 2), ("x1L", 3),
-    ("sib", 0, 1), ("r2z", 2, 1), ("comp", 0, 1), ("z2", 3, 0), ("r1bL", 2), ("r2z", 1, 1), ("r2z", 3, 0),
-    ("sib", 1, 0), ("r1bR", 1), ("z2", 3, 1), ("outer_end",), ("r2a",), ("sib", 3, 0), ("r1c", 0), ("x1F", 1),
-    ("x1F", 2), ("r1bL", 3), ("sib", 1, 1), ("comp", 1, 0), ("comp", 3, 0), ("x1F", 3), ("sib", 2, 0),
-    ("r2z", 3, 1), ("sib", 3, 1), ("r1bR", 3), ("comp", 1, 1), ("outer_mid",), ("r2bL",), ("r1c", 1), ("r1c", 2),
-    ("sib", 2, 1), ("comp", 2, 0), ("r2bR",), ("comp", 3, 1), ("comp", 2, 1), ("r1c", 3), ("r2c",),
+    ("o2x",), ("dw", 0), ("x1o", 0), ("o1z",), ("dw", 4), ("outer_send",), ("a2L",), ("dw", 1), ("a2R",), ("g2", 1),
+    ("pair", 4), ("pair", 0), ("z1", 1), ("r1a", 0), ("dw", 6), ("x1R", 0), ("z1", 2), ("x1o", 2), ("dw", 5),
+    ("dw", 3), ("x1L", 0), ("a2F",), ("dw", 7), ("g2", 0), ("dw", 2), ("r1a", 2), ("pair", 3), ("pair", 1),
+    ("z1", 3), ("pair", 5), ("sib", 0, 0), ("x1o", 1), ("x1o", 3), ("z2", 2, 1), ("pair", 2), ("pair", 7),
+    ("r2z", 0, 0), ("r1a", 1), ("outer_y",), ("pair", 6), ("x1F", 0), ("z2", 1, 1), ("comp", 0, 0), ("x1R", 2),
+    ("r1bL", 0), ("x1R", 1), ("z2", 2, 0), ("r1bR", 0), ("z2", 1, 0), ("x1L", 1), ("x1L", 3), ("z2", 3, 1),
+    ("x1L", 2), ("r2z", 1, 0), ("x1F", 1), ("x1R", 3), ("r2z", 2, 0), ("r2z", 0, 1), ("r1bR", 1), ("sib", 1, 0),
+    ("r1bL", 1), ("z2", 3, 0), ("r1a", 3), ("r2z", 1, 1), ("sib", 2, 0), ("r1bL", 2), ("sib", 1, 1), ("r1bR", 2),
+    ("x1F", 2), ("r2z", 3, 0), ("sib", 2, 1), ("r1c", 0), ("comp", 1, 0), ("r2a",), ("r2z", 2, 1), ("r1bL", 3),
+    ("comp", 1, 1), ("x1F", 3), ("comp", 2, 0), ("sib", 0, 1), ("r2z", 3, 1), ("r1bR", 3), ("r2bL",), ("sib", 3, 0),
+    ("comp", 2, 1), ("sib", 3, 1), ("r1c", 2), ("r1c", 1), ("r2bR",), ("outer_mid",), ("outer_end",),
+    ("comp", 3, 1), ("comp", 0, 1), ("comp", 3, 0), ("r1c", 3), ("r2c",),
 )
 ORDER = (ENDS, MIDDLE)
 
@@ -449,10 +450,16 @@
             "r2z": r2z_step, "r2a": r2a, "r2bL": r2bL, "r2bR": r2bR, "r2c": r2c,
             "outer_send": outer_send, "outer_y": outer_y, "outer_mid": outer_mid, "outer_end": outer_end,
         }
-        for name, *args in order:
+        issued, waited = [], 0
+        for step, (name, *args) in enumerate(order):
             actions[name](*args)
+            issued.append(len(pending_sends))
+            if step >= LAG:
+                for copy in pending_sends[waited:issued[step - LAG]]:
+                    copy.wait_send()
+                waited = issued[step - LAG]
         keys_o[...] = acc[...].astype(BF)
-        for copy in pending_sends:
+        for copy in pending_sends[waited:]:
             copy.wait_send()
 
     pl.when(low | high)(functools.partial(body, False, order[0]))

time: 65.3 us -> 63.2 us (0.968)
  Pallas kernels: 64.4 us -> 61.9 us
    pallas_call x1, Pallas kernels: 62.1 us -> 59.6 us  [launch(): pl.pallas_call(functools.partial(kernel, order, A1, R1), out_shape=[vm((T...]
where the time goes in v4:
time: 63.2 us; the launch traced here: 62.7 us
  Pallas kernels  61.9 us (98%)
  between operations  0.8 us (1%)
    pallas_call x1, Pallas kernels, launch(): pl.pallas_call(functools.partial(kernel, order, A1, R1), out_shape=[vm((T...  59.6 us
    pallas_call x1, Pallas kernels, launch(): pl.pallas_call(finish, out_shape=[jax.ShapeDtypeStruct(o.shape, o.dtype)...  2.33 us

profile of v4, /device:TPU:8, one launch (start us, length us, event | category | flops | bytes accessed | tf_op | source)
XLA Modules:
  0.0 62.7 jit_solution(4751719333623280172)
XLA Ops:
  0.6 59.6 %window.1 = (bf16[256,512]{1,0:T(8,128)(2,1)S(1)}, bf16[224,512]{1,0:T(8,128)(2,1)S(1)}, bf16[256,7168]{1,0:T(8,128)(2,1)S(1)}, bf16[224,1024]{1,0:T(8,128)(2,1)...) custom-call(bf16[256,7168]{1,0:T(8,128)(2,1)} %bitcast.8, ...), custom_call_target="tpu_custom_call" | custom-call | tf_op jit(solution)/shard_map/window/pallas_call | solution.py:489
  60.2 2.3 %finish.1 = (bf16[256,512]{1,0:T(8,128)(2,1)}, bf16[224,512]{1,0:T(8,128)(2,1)}, bf16[256,7168]{1,0:T(8,128)(2,1)}, bf16[224,1024]{1,0:T(8,128)(2,1)}, f32[224,1...) custom-call(bf16[256,512]{1,0:T(8,128)(2,1)S(1)} %get-tuple-element.21.refs_0_, ...), custom_call_target="tpu_custom_call" | custom-call | tf_op jit(solution)/shard_map/finish/pallas_call | solution.py:512

commit v5 on v4

--- a/solution.py
+++ b/solution.py
@@ -30,7 +30,8 @@
 for _name, _n in COUNTS:
     BASE[_name] = TOTAL
     TOTAL += _n
-LOADS = 7
+LOADS = 10
+QUARTER = TOK // 4
 LAG = 40
 
 
@@ -117,7 +118,9 @@
         remote(dst, dst, name, index, sibling).wait_recv()
 
     loads = [
-        (kw_h, w.at[(*chip(z, x), c)]), (cot_h, cot), (acts_h, acts), (fl_h, fl),
+        (kw_h, w.at[(*chip(z, x), c)]), (cot_h, cot),
+        *[(acts_h.at[pl.ds(k * QUARTER, QUARTER)], acts.at[pl.ds(k * QUARTER, QUARTER)]) for k in range(4)],
+        (fl_h, fl),
         (anchor_h, anchor), (moment_h, moment), (pending_h, pending),
     ]
     loads = [pltpu.make_async_copy(s, t, load_sem.at[i]) for i, (s, t) in enumerate(loads)]
@@ -241,8 +244,8 @@
 
         def await_tokens():
             if not tokens_here:
-                loads[1].wait()
-                loads[2].wait()
+                for copy in loads[1:6]:
+                    copy.wait()
                 tokens_here.append(True)
 
         def comp(j, p):
@@ -392,7 +395,7 @@
             grad_o[pl.ds(R1, R2)] = (total * scale).astype(BF)
 
         def outer_send():
-            for copy in loads[3:]:
+            for copy in loads[6:]:
                 copy.wait()
             for k in range(1, 4):
                 ty = (y + k) % 4

time: 63.2 us -> 63.2 us (level)
  no operation moved by 1% of the time
where the time goes in v5:
time: 63.2 us; the launch traced here: 62.7 us
  Pallas kernels  61.9 us (98%)
  between operations  0.8 us (1%)
    pallas_call x1, Pallas kernels, launch(): pl.pallas_call(functools.partial(kernel, order, A1, R1), out_shape=[vm((T...  59.6 us
    pallas_call x1, Pallas kernels, launch(): pl.pallas_call(finish, out_shape=[jax.ShapeDtypeStruct(o.shape, o.dtype)...  2.33 us

profile of v5, /device:TPU:8, one launch (start us, length us, event | category | flops | bytes accessed | tf_op | source)
XLA Modules:
  0.0 62.7 jit_solution(14189697768121916074)
XLA Ops:
  0.6 59.6 %window.1 = (bf16[256,512]{1,0:T(8,128)(2,1)S(1)}, bf16[224,512]{1,0:T(8,128)(2,1)S(1)}, bf16[256,7168]{1,0:T(8,128)(2,1)S(1)}, bf16[224,1024]{1,0:T(8,128)(2,1)...) custom-call(bf16[256,7168]{1,0:T(8,128)(2,1)} %bitcast.8, ...), custom_call_target="tpu_custom_call" | custom-call | tf_op jit(solution)/shard_map/window/pallas_call | solution.py:492
  60.3 2.3 %finish.1 = (bf16[256,512]{1,0:T(8,128)(2,1)}, bf16[224,512]{1,0:T(8,128)(2,1)}, bf16[256,7168]{1,0:T(8,128)(2,1)}, bf16[224,1024]{1,0:T(8,128)(2,1)}, f32[224,1...) custom-call(bf16[256,512]{1,0:T(8,128)(2,1)S(1)} %get-tuple-element.21.refs_0_, ...), custom_call_target="tpu_custom_call" | custom-call | tf_op jit(solution)/shard_map/finish/pallas_call | solution.py:515
